TPU v7x, 512 devices: a whole 4x4x16 slice. The times are simulated.
512 devices in a mesh: mesh: 64 (over y, z), mem: 8 (over x, core).
Axes of the slice: x: 4, y: 4, z: 16, core: 2. Of those that a mesh axis runs over, the one named last changes fastest.
Arguments:
- ensemble: bfloat16 [40, 240, 24576], P('mem', None, 'mesh'), may hold values from -6 to 6
- ovl_owner: int32 [1536, 2], P('mesh'), may hold values from 0 to 63, all different within a row; in each aligned block of 24 rows (0 to 23, 24 to 47, ...) at most 2 rows name the same one
- ovl_patch: int32 [1536, 2], P('mesh'), may hold values from 0 to 7
- ovl_weight: bfloat16 [1536, 2, 16, 8], P('mesh'), may hold values from 0.0099487305 to 0.19921875
- letkf_weight: float32 [64, 40, 40], P('mesh'), may hold values from -1 to 1
Outputs:
- analysis: bfloat16 [40, 240, 24576], P('mem', None, 'mesh')
Inputs may be any that keep to these rules, and one draw needn't show every extreme that they name: `ovl_owner`: within the 24 rows of one mesh index, the two entries of a row differ, and each owner is named at most 2 times; some owner exactly 2 times.
All inputs are finite; a program needn't handle non-finite values.
Results may differ from a plain program's by a relative error of at most 0.0015.
Values may be sent and summed in bfloat16 or wider, within the bound.
No kernel may reach another device: no remote copies, remote signals or barrier semaphores. Data moves between devices by JAX's collectives and lax.ppermute only.
A program may use at most 128 MiB of HBM per device.

v0:
```python
import math

import jax
import jax.numpy as jnp
from jax import lax
from jax.sharding import PartitionSpec as P

PATCH_TILE = 8


def side_by_side(arrays, axis, split_dim, concat_dim, along):
    widths = [math.prod(a.shape[along:]) for a in arrays]
    both = jnp.concatenate(
        [a.reshape(*a.shape[:along], w) for a, w in zip(arrays, widths)], axis=along
    )
    whole = lax.all_to_all(both, axis, split_axis=split_dim, concat_axis=concat_dim, tiled=True)
    blocks = jnp.split(whole, [sum(widths[:k]) for k in range(1, len(widths))], axis=along)
    return tuple(
        (b.reshape(*whole.shape[:along], *a.shape[along:]) for a, b in zip(arrays, blocks))
    )


def copy_for_each(value, axis):
    copies = jnp.broadcast_to(value, (lax.axis_size(axis), *value.shape))
    return lax.all_to_all(copies, axis, split_axis=0, concat_axis=0, tiled=True)


def in_order(blocks, dim):
    blocks = jnp.moveaxis(blocks, 0, dim)
    dims = blocks.shape
    return blocks.reshape(*dims[:dim], dims[dim] * dims[dim + 1], *dims[dim + 2 :])


def gathered_copies(value, axis, dim):
    blocks = copy_for_each(value, axis)
    return in_order(blocks, dim)


def patch_grid(contribution, slot_margin, slot_codes, patch_count):
    slot_total = contribution.shape[0]
    assign = (
        jnp.arange(1, patch_count + 1, dtype=jnp.int32)[:, None]
        == slot_codes.reshape(-1).astype(jnp.int32)[None, :]
    )
    assign_half = assign.astype(jnp.bfloat16)
    patch_sums = jnp.dot(
        assign_half, contribution.reshape(slot_total, -1), preferred_element_type=jnp.float32
    )
    patch_sums = patch_sums.reshape((patch_count,) + contribution.shape[1:])
    column_sums = jnp.sum(slot_margin.astype(jnp.float32), axis=1)
    coverage = jnp.dot(assign.astype(jnp.float32), column_sums, precision=lax.Precision.HIGHEST)
    grid_field = (patch_sums / jnp.maximum(coverage, 1.0)[:, :, None, None]).astype(jnp.bfloat16)
    return (grid_field, assign_half)


def shards(ensemble, ovl_owner, ovl_patch, ovl_weight, letkf_weight):
    members, channels, element_count = ensemble.shape
    block_count = ovl_owner.shape[0]
    block_size = ovl_weight.shape[2]
    cell_count = ovl_weight.shape[3]
    tile_count = letkf_weight.shape[0]
    patch_count = tile_count * PATCH_TILE
    peer_count = lax.axis_size("mesh")
    capacity = max(2, (3 * block_count + peer_count - 1) // peer_count)
    slot_total = peer_count * capacity
    piece_count = 2 * block_count
    blocks = ensemble.reshape(members, channels, block_count, block_size)
    owners = ovl_owner.reshape(-1)
    patches = ovl_patch.reshape(-1)
    positions = jnp.arange(piece_count, dtype=jnp.int32)
    same_owner = owners[:, None] == owners[None, :]
    earlier = positions[:, None] > positions[None, :]
    ranking = jnp.sum(jnp.where(same_owner & earlier, 1, 0), axis=1).astype(jnp.int32)
    slot_index = owners * capacity + ranking
    selector = (jnp.arange(slot_total, dtype=jnp.int32)[:, None] == slot_index[None, :]).astype(
        jnp.bfloat16
    )
    codes = (patches + 1).astype(jnp.bfloat16)[:, None]
    slot_codes = (
        jnp.dot(selector, codes, preferred_element_type=jnp.float32)
        .astype(jnp.bfloat16)
        .reshape(peer_count, capacity)
    )
    weight_flat = ovl_weight.reshape(piece_count, block_size * cell_count)
    slot_weight = jnp.dot(selector, weight_flat, preferred_element_type=jnp.float32).astype(
        jnp.bfloat16
    )
    slot_weight = slot_weight.reshape(peer_count, capacity, block_size * cell_count)
    formed = jnp.einsum("mcbe,bkeg->bkgmc", blocks, ovl_weight, preferred_element_type=jnp.float32)
    payload = formed.astype(jnp.bfloat16).reshape(piece_count, -1)
    slot_data = jnp.dot(selector, payload, preferred_element_type=jnp.float32).astype(jnp.bfloat16)
    slot_data = slot_data.reshape(peer_count, capacity, -1)
    got_data, got_weight, got_codes = side_by_side(
        (slot_data, slot_weight, slot_codes), "mesh", 0, 0, 2
    )
    slot_margin = got_weight.reshape(slot_total, block_size, cell_count)
    contribution = got_data.reshape(slot_total, cell_count, members, channels)
    grid_field, assign_half = patch_grid(contribution, slot_margin, got_codes, patch_count)
    tile_view = grid_field.reshape(tile_count, PATCH_TILE, cell_count, members, channels)
    own_start = lax.axis_index("mem") * members
    own_cols = lax.dynamic_slice_in_dim(letkf_weight, own_start, members, 2)
    mixed = jnp.einsum(
        "tjgmc,tmn->tjgnc",
        gathered_copies(tile_view, "mem", 3).astype(jnp.float32),
        own_cols,
        precision=lax.Precision.HIGHEST,
    )
    increment = (mixed - tile_view.astype(jnp.float32)).astype(jnp.bfloat16)
    increment_flat = increment.reshape(patch_count, -1)
    send_back = jnp.dot(assign_half.T, increment_flat, preferred_element_type=jnp.float32).astype(
        jnp.bfloat16
    )
    send_back = send_back.reshape(peer_count, capacity, -1)
    returned = lax.all_to_all(send_back, "mesh", split_axis=0, concat_axis=0, tiled=True)
    returned_flat = returned.reshape(slot_total, -1)
    own_pieces = jnp.dot(selector.T, returned_flat, preferred_element_type=jnp.float32).astype(
        jnp.bfloat16
    )
    own_pieces = own_pieces.reshape(block_count, 2, cell_count, members, channels)
    element_area = jnp.sum(ovl_weight.astype(jnp.float32), axis=(1, 3))
    correction = jnp.einsum(
        "bkgmc,bkeg->mcbe", own_pieces, ovl_weight, preferred_element_type=jnp.float32
    )
    correction = correction / element_area[None, None]
    updated = (blocks.astype(jnp.float32) + correction).astype(jnp.bfloat16)
    return updated.reshape(members, channels, element_count)


def solution(mesh):
    in_specs = (
        P("mem", None, "mesh"),
        P("mesh", None),
        P("mesh", None),
        P("mesh", None, None, None),
        P("mesh", None, None),
    )
    out_specs = P("mem", None, "mesh")
    return jax.shard_map(shards, mesh=mesh, in_specs=in_specs, out_specs=out_specs, check_vma=False)
```

profile of v0, /device:TPU:32, one launch (start us, length us, event | category | flops | bytes accessed | tf_op | source)
XLA Modules:
  0.0 337.5 jit_solution(15104423322569973558)
XLA Ops:
  1.1 1.6 copy.59
  2.7 1.8 copy.65
  6.3 1.6 reshape.85
  7.9 2.2 convolution_convert_fusion.1
  10.1 2.9 reshape.86
  14.9 4.0 %pad_maximum_fusion = bf16[64,2,9729]{2,1,0:T(2,128)(2,1)} fusion(bf16[64,2,1]{2,1,0:T(2,128)(2,1)S(1)} %reshape_reshape.9, bf16[64,2,128]{2,1,0:T(2,128)(2,1)S(1)} %bitcast.64, bf16[64,2,9600]{2,1,0:T(2,128)(2,1)S(1)} %reshape.86), kind=kLoop, calls=%fused_computation.3 | loop fusion | flops 7471872 | bytes 4981248 | tf_op jit(solution)/shard_map/concatenate | solution.py:13
  18.9 18.4 %all-to-all-start = ((bf16[64,2,9729]{2,1,0:T(2,128)(2,1)}), bf16[64,2,9729]{2,1,0:T(2,128)(2,1)S(1)}, u32[]{:S(2)}, u32[]{:S(2)}) async-start(bf16[64,2,9729]{2,1,0:T(2,128)(2,1)} %pad_maximum_fusion), calls=%async_computation | async-start | bytes 5046272 | tf_op jit(solution)/shard_map/all_to_all | solution.py:16
  37.3 116.5 %all-to-all-done = bf16[64,2,9729]{2,1,0:T(2,128)(2,1)S(1)} async-done(((bf16[64,2,9729]{2,1,0:T(2,128)(2,1)}), bf16[64,2,9729]{2,1,0:T(2,128)(2,1)S(1)}, u32[]{:S(2)}, u32[]{:S(2)}) %all-to-all-start) | async-done | bytes 2490656 | tf_op jit(solution)/shard_map/all_to_all | solution.py:16
  153.8 1.8 convert_reduce_fusion.1
  157.2 2.4 reshape.97
  159.6 2.1 reduce_sum.28
  162.7 3.2 split.13
  165.9 4.3 %reshape_reshape.8 = bf16[128,9600]{1,0:T(8,128)(2,1)} reshape(bf16[64,2,9600]{2,1,0:T(2,128)(2,1)} %split.13) | data formatting | bytes 4915200 | tf_op jit(solution)/shard_map/reshape;reshape | solution.py:47
  170.2 3.9 %copy.69 = bf16[9600,128]{1,0:T(8,128)(2,1)S(1)} copy(bf16[9600,128]{0,1:T(8,128)(2,1)} %bitcast.57) | data formatting | bytes 4915200 | tf_op jit(solution)/shard_map/dot_general | solution.py:46
  177.4 4.3 %all-to-all-start.1 = ((bf16[8,1,8,8,5,240]{5,3,4,2,1,0:T(8,128)(2,1)}), bf16[8,1,8,8,5,240]{5,3,4,2,1,0:T(8,128)(2,1)S(1)}, u32[]{:S(2)}, u32[]{:S(2)}) async-start(bf16[8,1,8,8,5,240]{5,3,4,2,1,0:T(8,128)(2,1)} %broadcast_in_dim.12), calls=%async_computation.1 | async-start | bytes 2621440 | tf_op jit(solution)/shard_map/all_to_all | solution.py:25
  181.7 18.8 %all-to-all-done.1 = bf16[8,1,8,8,5,240]{5,3,4,2,1,0:T(8,128)(2,1)S(1)} async-done(((bf16[8,1,8,8,5,240]{5,3,4,2,1,0:T(8,128)(2,1)}), bf16[8,1,8,8,5,240]{5,3,4,2,1,0:T(8,128)(2,1)S(1)}, u32[]{:S(2)}, u32[]{:S(2)}) %all-to-all-start.1) | async-done | bytes 1228832 | tf_op jit(solution)/shard_map/all_to_all | solution.py:25
  202.6 1.8 convolution_convert_fusion
  204.4 2.4 reshape.92
  206.8 7.5 %all-to-all-start.2 = ((bf16[64,2,9600]{2,1,0:T(2,128)(2,1)}), bf16[64,2,9600]{2,1,0:T(2,128)(2,1)S(1)}, u32[]{:S(2)}, u32[]{:S(2)}) async-start(bf16[64,2,9600]{2,1,0:T(2,128)(2,1)} %reshape.92), calls=%async_computation.2 | async-start | bytes 4915200 | tf_op jit(solution)/shard_map/all_to_all | solution.py:114
  215.2 112.5 %all-to-all-done.2 = bf16[64,2,9600]{2,1,0:T(2,128)(2,1)S(1)} async-done(((bf16[64,2,9600]{2,1,0:T(2,128)(2,1)}), bf16[64,2,9600]{2,1,0:T(2,128)(2,1)S(1)}, u32[]{:S(2)}, u32[]{:S(2)}) %all-to-all-start.2) | async-done | bytes 2457632 | tf_op jit(solution)/shard_map/all_to_all | solution.py:114
  327.7 2.4 reshape.93
  330.1 2.2 convolution_convert_fusion.2
  332.3 2.2 reshape.94
  334.6 1.5 fusion
  (42 shorter events, 15.1 us)
Async XLA Ops:
  0.0 200.6 %copy-start = (f32[1,40,40]{2,1,0:T(8,128)S(1)}, f32[1,40,40]{2,1,0:T(8,128)}, u32[]{:S(2)}) copy-start(f32[1,40,40]{2,1,0:T(8,128)} %param.9) | copy-start | bytes 19204
  10.1 4.2 %copy-start.4 = (s32[24,2]{0,1:T(2,128)S(1)}, s32[24,2]{0,1:T(2,128)}, u32[]{:S(2)}) copy-start(s32[24,2]{0,1:T(2,128)} %param.7) | copy-start | bytes 580
  18.9 134.9 %all-to-all-start = ((bf16[64,2,9729]{2,1,0:T(2,128)(2,1)}), bf16[64,2,9729]{2,1,0:T(2,128)(2,1)S(1)}, u32[]{:S(2)}, u32[]{:S(2)}) async-start(bf16[64,2,9729]{2,1,0:T(2,128)(2,1)} %pad_maximum_fusion), calls=%async_computation | async-start | bytes 5046272 | tf_op jit(solution)/shard_map/all_to_all | solution.py:16
  175.5 0.7 copy-start.1
  177.4 23.1 %all-to-all-start.1 = ((bf16[8,1,8,8,5,240]{5,3,4,2,1,0:T(8,128)(2,1)}), bf16[8,1,8,8,5,240]{5,3,4,2,1,0:T(8,128)(2,1)S(1)}, u32[]{:S(2)}, u32[]{:S(2)}) async-start(bf16[8,1,8,8,5,240]{5,3,4,2,1,0:T(8,128)(2,1)} %broadcast_in_dim.12), calls=%async_computation.1 | async-start | bytes 2621440 | tf_op jit(solution)/shard_map/all_to_all | solution.py:25
  181.7 19.7 %copy-start.2 = (bf16[8,8,5,240]{3,0,2,1:T(8,128)(2,1)S(1)}, bf16[8,8,5,240]{3,0,2,1:T(8,128)(2,1)}, u32[]{:S(2)}) copy-start(bf16[8,8,5,240]{3,0,2,1:T(8,128)(2,1)} %copy-done.1) | copy-start | bytes 460804
  206.8 7.5 %copy-start.3 = (bf16[24,2,16,8]{0,3,2,1:T(8,128)(2,1)S(1)}, bf16[24,2,16,8]{0,3,2,1:T(8,128)(2,1)}, u32[]{:S(2)}) copy-start(bf16[24,2,16,8]{0,3,2,1:T(8,128)(2,1)} %param.8) | copy-start | bytes 36868
  206.8 120.9 %all-to-all-start.2 = ((bf16[64,2,9600]{2,1,0:T(2,128)(2,1)}), bf16[64,2,9600]{2,1,0:T(2,128)(2,1)S(1)}, u32[]{:S(2)}, u32[]{:S(2)}) async-start(bf16[64,2,9600]{2,1,0:T(2,128)(2,1)} %reshape.92), calls=%async_computation.2 | async-start | bytes 4915200 | tf_op jit(solution)/shard_map/all_to_all | solution.py:114
where the time goes:
time: 339 us; the launch traced here: 338 us
  waiting for transfers between devices  248 us (73%)
  local copies, waits for them, and re-layouts  38.9 us (11%)
  starting transfers between devices  30.2 us (9%)
  matrix products  11.6 us (3%)
  other arithmetic  8.91 us (3%)
    all_to_all x1, waiting for transfers between devices, side_by_side(): lax.all_to_all(both, axis, split_axis=split_dim, concat_axis=concat_dim,...  116 us
    all_to_all x1, waiting for transfers between devices, shards(): lax.all_to_all(send_back, 'mesh', split_axis=0, concat_axis=0, tiled=True)  112 us
    all_to_all x1, waiting for transfers between devices, copy_for_each(): return lax.all_to_all(copies, axis, split_axis=0, concat_axis=0, tiled=True)  18.8 us
    all_to_all x1, starting transfers between devices, side_by_side(): lax.all_to_all(both, axis, split_axis=split_dim, concat_axis=concat_dim,...  18.4 us
    all_to_all x1, starting transfers between devices, shards(): lax.all_to_all(send_back, 'mesh', split_axis=0, concat_axis=0, tiled=True)  7.5 us
  transfers between devices with their start and end apart: 3, of which 3 were waited for; matrix products, arithmetic and copies ran while one was open for 0% of the time, Pallas kernels for 0%

commit v1 on v0

v1 whole, which is shorter than its diff:
```python
import jax
import jax.numpy as jnp
from jax import lax
from jax.experimental import pallas as pl
from jax.experimental.pallas import tpu as pltpu
from jax.sharding import PartitionSpec as P

MESH = 64
MEM = 8
MEMBERS = 5
CHANNELS = 240
ELEMENTS = 384
CELLS = 8
PATCHES = 512
ROWS = 16
THIRDS = 3
WIDTH = 512
SIDE = 96
COLUMNS = 160
BF = jnp.bfloat16
F32 = jnp.float32
VMEM_BYTES = 40 * 1024 * 1024


def iota(shape, dim):
    return lax.broadcasted_iota(jnp.int32, shape, dim)


def dot(a, b):
    return jnp.dot(a, b, preferred_element_type=F32)


def dot_nt(a, b):
    return lax.dot_general(a, b, (((1,), (1,)), ((), ())), preferred_element_type=F32)


def one_hot(mask):
    return jnp.where(mask, 1.0, 0.0).astype(BF)


def member_tiles(group):
    return [(half, m, group * 32 + half * 16) for half in range(2) for m in range(MEMBERS)]


def source_kernel(mem_ref, ens_ref, margin_ref, owner_ref, patch_ref, letkf_ref, out_ref, spread_ref):
    lane24 = iota((24, ELEMENTS), 1)
    block_of = (lane24 // 128) * 8 + lane24 % 8
    pick_block = iota((24, ELEMENTS), 0) == block_of
    expanded = dot(margin_ref[...], one_hot(pick_block))
    row = iota((256, ELEMENTS), 0)
    lane = iota((256, ELEMENTS), 1)
    fits = (row // 128 == (lane % 16) // 8) & (row % 8 == (lane % 128) // 16)
    expanded = jnp.where(fits, expanded, 0.0).astype(BF)
    fold = one_hot((iota((ELEMENTS, 256), 1) % 128) // 8 == iota((ELEMENTS, 256), 0) % 16)
    spread = dot(fold, expanded)
    er = iota((ELEMENTS, ELEMENTS), 0)
    el = iota((ELEMENTS, ELEMENTS), 1)
    spread = jnp.where(er // 16 == (el // 128) * 8 + el % 8, spread, 0.0)
    sums = jnp.sum(spread, axis=0, keepdims=True)
    spread = spread.astype(BF)
    spread_ref[...] = spread
    high = sums.astype(BF).astype(F32)
    low = sums - high

    dest = owner_ref[...] * 8 + patch_ref[...] - 256
    dest = dest.astype(F32).astype(BF)
    place = dot(dest, one_hot(pick_block))
    lane2 = iota((2, ELEMENTS), 1)
    place = jnp.sum(jnp.where((lane2 % 16) // 8 == iota((2, ELEMENTS), 0), place, 0.0), axis=0, keepdims=True)

    own = mem_ref[0] * MEMBERS
    pick_own = one_hot((iota((16, 40), 1) == own + iota((16, 40), 0) // 3) & (iota((16, 40), 0) < 15))
    mine = dot_nt(pick_own, letkf_ref[...].astype(BF))
    keep = (iota((16, 40), 1) // 16) == iota((16, 40), 0) % 3
    mine = jnp.where(keep, mine, 0.0).astype(BF)
    weights = dot(mine, one_hot(iota((40, 128), 0) % 16 == iota((40, 128), 1) % 16))

    def parts(value):
        return [value[:, 128 * h : 128 * h + 128] for h in range(THIRDS)]

    side = jnp.concatenate(
        parts(place) + parts(high) + parts(low) + [jnp.zeros((7, 128), F32), weights], axis=0
    )

    for group in range(8):
        tiles = []
        for half, m, start in member_tiles(group):
            if start < CHANNELS:
                tiles.append(ens_ref[m, start : start + 16, :])
            else:
                tiles.append(jnp.zeros((16, ELEMENTS), BF))
        pieces = dot(jnp.concatenate(tiles, axis=0), spread)
        for h in range(THIRDS):
            block = pieces[0:128, 128 * h : 128 * h + 128].T.astype(BF)
            out_ref[8 * group : 8 * group + 8, :, 128 * h : 128 * h + 128] = block.reshape(8, ROWS, 128)
        rest = jnp.concatenate(parts(pieces[128:160]) + [side], axis=0)
        out_ref[8 * group : 8 * group + 8, :, 384:512] = rest.T.astype(BF).reshape(8, ROWS, 128)


def hits(side, h):
    place = side[:, SIDE + h : SIDE + h + 1].astype(F32) + 256.0
    lanes = iota((MESH * ROWS, PATCHES), 1).astype(F32)
    return one_hot(lanes == place)


def patch_kernel(got_ref, out_ref, weight_ref):
    got = got_ref[...].reshape(MESH * ROWS, WIDTH)
    last = got[:, 384:512].astype(F32)
    last_t = last.T.astype(BF)
    total = jnp.zeros((128, PATCHES), F32)
    rest = jnp.zeros((32, PATCHES), F32)
    cover = jnp.zeros((1, PATCHES), F32)
    for h in range(THIRDS):
        first_t = got[:, 128 * h : 128 * h + 128].astype(F32).T.astype(BF)
        left = jnp.concatenate([first_t, last_t[32 * h : 32 * h + 32], last_t[96:112]], axis=0)
        sums = dot(left, hits(last, h))
        total = total + sums[0:128]
        rest = rest + sums[128:160]
        cover = cover + sums[163 + h : 164 + h] + sums[166 + h : 167 + h]
    cover = jnp.maximum(cover, 1.0)
    total = (total / cover).astype(BF)
    rest = (rest / cover).astype(BF)
    for q in range(MEM):
        out_ref[q, 0:128, :] = total
        out_ref[q, 128:160, :] = rest

    wide = last_t[112:128]
    lane = iota((ROWS, MESH * ROWS), 1)
    rows = jnp.concatenate(
        [jnp.where(lane % 16 == r, wide, jnp.zeros_like(wide)) for r in range(ROWS)], axis=0
    )
    tile = one_hot(
        iota((MESH * ROWS, PATCHES), 0) // 16 == iota((MESH * ROWS, PATCHES), 1) // 8
    )
    weight_ref[...] = dot(rows, tile)


def mixing_kernel(grid_ref, own_ref, weight_ref, got_ref, out_ref, inc_ref):
    for half in range(2):
        for lanes in range(PATCHES // 128):
            at = slice(128 * lanes, 128 * lanes + 128)
            mixed = [jnp.zeros((16, 128), F32) for _ in range(MEMBERS)]
            for m in range(MEM * MEMBERS):
                row = (half * MEMBERS + m % MEMBERS) * 16
                field = grid_ref[m // MEMBERS, row : row + 16, at].astype(F32)
                for n in range(MEMBERS):
                    w = (m % 16) * 16 + n * 3 + m // 16
                    mixed[n] = mixed[n] + weight_ref[w : w + 1, at] * field
            for n in range(MEMBERS):
                row = (half * MEMBERS + n) * 16
                inc_ref[row : row + 16, at] = mixed[n] - own_ref[0, row : row + 16, at].astype(F32)
    side = got_ref[...].reshape(MESH * ROWS, 128).astype(F32)
    first = inc_ref[0:128, :].T.astype(BF)
    small = inc_ref[128:160, :]
    last = jnp.zeros((MESH * ROWS, 128), F32)
    for h in range(THIRDS):
        pad = [jnp.zeros((32, PATCHES), F32)] * 4
        pad[h] = small
        right = jnp.concatenate([first, jnp.concatenate(pad, axis=0).T.astype(BF)], axis=1)
        back = dot(hits(side, h), right)
        out_ref[:, :, 128 * h : 128 * h + 128] = back[:, 0:128].astype(BF).reshape(MESH, ROWS, 128)
        last = last + back[:, 128:256]
    out_ref[:, :, 384:512] = last.astype(BF).reshape(MESH, ROWS, 128)


def final_kernel(back_ref, ens_ref, spread_ref, out_ref):
    spread = spread_ref[...]
    area = dot_nt(jnp.ones((16, ELEMENTS), BF), spread)[0:1]
    scale = 1.0 / area
    for group in range(8):
        def turned(k):
            block = back_ref[8 * group : 8 * group + 8, :, 128 * k : 128 * k + 128]
            return block.reshape(128, 128).astype(F32).T

        first = jnp.concatenate([turned(h) for h in range(THIRDS)], axis=1)
        last = turned(3)
        last = jnp.concatenate([last[32 * h : 32 * h + 32] for h in range(THIRDS)], axis=1)
        left = jnp.concatenate([first, last], axis=0).astype(BF)
        correction = dot_nt(left, spread) * scale
        for k, (half, m, start) in enumerate(member_tiles(group)):
            if start < CHANNELS:
                value = ens_ref[m, start : start + 16, :].astype(F32) + correction[16 * k : 16 * k + 16]
                out_ref[m, start : start + 16, :] = value.astype(BF)


def vmem():
    return pl.BlockSpec(memory_space=pltpu.VMEM)


def call(kernel, outs, ins, scratch=()):
    return pl.pallas_call(
        kernel,
        out_shape=[jax.ShapeDtypeStruct(s, d) for s, d in outs],
        in_specs=ins,
        out_specs=[vmem() for _ in outs],
        scratch_shapes=list(scratch),
        compiler_params=pltpu.CompilerParams(vmem_limit_bytes=VMEM_BYTES),
    )


def shards(ensemble, ovl_owner, ovl_patch, ovl_weight, letkf_weight):
    margin = ovl_weight.transpose(1, 2, 3, 0).reshape(256, 24)
    mem = lax.axis_index("mem").astype(jnp.int32).reshape(1)
    send, spread = call(
        source_kernel,
        [((MESH, ROWS, WIDTH), BF), ((ELEMENTS, ELEMENTS), BF)],
        [pl.BlockSpec(memory_space=pltpu.SMEM)] + [vmem()] * 5,
    )(mem, ensemble, margin, ovl_owner.T, ovl_patch.T, letkf_weight[0])
    got = lax.all_to_all(send, "mesh", split_axis=0, concat_axis=0, tiled=True)
    copies, weight = call(
        patch_kernel, [((MEM, COLUMNS, PATCHES), BF), ((256, PATCHES), F32)], [vmem()]
    )(got)
    grid = lax.all_to_all(copies, "mem", split_axis=0, concat_axis=0, tiled=True)
    (back,) = call(
        mixing_kernel,
        [((MESH, ROWS, WIDTH), BF)],
        [vmem()] * 4,
        [pltpu.VMEM((COLUMNS, PATCHES), F32)],
    )(grid, copies[0:1], weight, got[:, :, 384:512])
    returned = lax.all_to_all(back, "mesh", split_axis=0, concat_axis=0, tiled=True)
    (analysis,) = call(final_kernel, [((MEMBERS, CHANNELS, ELEMENTS), BF)], [vmem()] * 3)(
        returned, ensemble, spread
    )
    return analysis


def solution(mesh):
    in_specs = (
        P("mem", None, "mesh"),
        P("mesh", None),
        P("mesh", None),
        P("mesh", None, None, None),
        P("mesh", None, None),
    )
    out_specs = P("mem", None, "mesh")
    return jax.shard_map(shards, mesh=mesh, in_specs=in_specs, out_specs=out_specs, check_vma=False)
```

time: 339 us -> 169 us (0.50)
  the two profiles are of different devices: /device:TPU:32 before, /device:TPU:8 now
where the time goes in v1:
time: 169 us; the launch traced here: 168 us
  blocking collectives  133 us (79%)
  waiting for transfers between devices  17.8 us (11%)
  Pallas kernels  7.23 us (4%)
  local copies, waits for them, and re-layouts  6.18 us (4%)
  starting transfers between devices  4.3 us (3%)
    all_to_all x1, blocking collectives, shards(): got = lax.all_to_all(send, 'mesh', split_axis=0, concat_axis=0, tiled=True)  72.3 us
    all_to_all x1, blocking collectives, shards(): lax.all_to_all(back, 'mesh', split_axis=0, concat_axis=0, tiled=True)  60.3 us
    all_to_all x1, waiting for transfers between devices, shards(): lax.all_to_all(copies, 'mem', split_axis=0, concat_axis=0, tiled=True)  17.8 us
    unnamed x18, local copies, waits for them, and re-layouts  5.2 us
    all_to_all x1, starting transfers between devices, shards(): lax.all_to_all(copies, 'mem', split_axis=0, concat_axis=0, tiled=True)  4.3 us
  transfers between devices with their start and end apart: 1, of which 1 were waited for; matrix products, arithmetic and copies ran while one was open for 1% of the time, Pallas kernels for 0%

profile of v1, /device:TPU:8, one launch (start us, length us, event | category | flops | bytes accessed | tf_op | source)
XLA Modules:
  0.0 168.2 jit_solution(10712047952162267209)
XLA Ops:
  0.0 0.0 copy-start
  0.0 1.2 copy-done
  1.2 0.8 copy-done.5
  2.0 0.7 copy-done.6
  2.8 0.7 copy-done.7
  3.4 0.7 copy-done.8
  4.1 1.4 shard_map.55
  5.5 0.0 copy-start.3
  5.5 72.3 %all_to_all.15.got_ref = bf16[64,16,512]{2,1,0:T(8,128)(2,1)S(1)} all-to-all(bf16[64,16,512]{2,1,0:T(8,128)(2,1)S(1)} %get-tuple-element.9), channel_id=1, replica_groups=mesh['mesh'=64,'mem'=8] {'mesh'}, dimensions={0} | all-to-all | bytes 2097152 | tf_op jit(solution)/shard_map/all_to_all | solution.py:209
  77.8 1.5 shard_map.56
  79.3 0.0 copy-done.3
  79.3 0.0 copy-start.2
  79.3 1.1 copy-done.2
  80.4 4.3 %all-to-all-start.1 = ((bf16[8,160,512]{2,1,0:T(8,128)(2,1)}), bf16[8,160,512]{2,1,0:T(8,128)(2,1)S(1)}, u32[]{:S(2)}, u32[]{:S(2)}) async-start(bf16[8,160,512]{2,1,0:T(8,128)(2,1)} %copy-done.2), calls=%async_computation.1 | async-start | bytes 2621440 | tf_op jit(solution)/shard_map/all_to_all | solution.py:213
  84.7 0.9 slice.6.own_ref
  85.6 0.1 slice.8.got_ref
  85.7 17.8 %all-to-all-done.1.grid_ref = bf16[8,160,512]{2,1,0:T(8,128)(2,1)S(1)} async-done(((bf16[8,160,512]{2,1,0:T(8,128)(2,1)}), bf16[8,160,512]{2,1,0:T(8,128)(2,1)S(1)}, u32[]{:S(2)}, u32[]{:S(2)}) %all-to-all-start.1) | async-done | bytes 1310752 | tf_op jit(solution)/shard_map/all_to_all | solution.py:213
  103.5 2.4 %shard_map.57 = bf16[64,16,512]{2,1,0:T(8,128)(2,1)S(1)} custom-call(bf16[8,160,512]{2,1,0:T(8,128)(2,1)S(1)} %all-to-all-done.1.grid_ref, bf16[1,160,512]{2,1,0:T(8,128)(2,1)S(1)} %slice.6.own_ref, f32[256,512]{1,0:T(8,128)S(1)} %get-tuple-element.11.weight_ref, bf16[64,16,128]{2,1,0:T(8,128)(2,1)S(1)} %slice.8.got_ref), custom_call_target="tpu_custom_call" | custom-call | tf_op jit(solution)/shard_map/pallas_call | solution.py:214
  105.9 0.0 copy-start.1
  105.9 0.0 copy-start.4
  105.9 60.3 %all_to_all.16.back_ref = bf16[64,16,512]{2,1,0:T(8,128)(2,1)S(1)} all-to-all(bf16[64,16,512]{2,1,0:T(8,128)(2,1)S(1)} %shard_map.57), channel_id=1, replica_groups=mesh['mesh'=64,'mem'=8] {'mesh'}, dimensions={0} | all-to-all | bytes 2097152 | tf_op jit(solution)/shard_map/all_to_all | solution.py:220
  166.3 0.0 copy-done.1
  166.3 0.0 copy-done.4
  166.3 2.0 %shard_map.58 = bf16[5,240,384]{2,1,0:T(8,128)(2,1)} custom-call(bf16[64,16,512]{2,1,0:T(8,128)(2,1)S(1)} %all_to_all.16.back_ref, bf16[5,240,384]{2,1,0:T(8,128)(2,1)S(1)} %copy-done.1, bf16[384,384]{1,0:T(8,128)(2,1)S(1)} %copy-done.4), custom_call_target="tpu_custom_call" | custom-call | tf_op jit(solution)/shard_map/pallas_call | solution.py:221
  (4 shorter events, 0.0 us)
Async XLA Ops:
  0.0 1.2 copy-start
  1.2 0.8 copy-start.5
  2.0 0.7 copy-start.6
  2.7 0.7 copy-start.7
  3.4 0.7 copy-start.8
  5.5 73.8 %copy-start.3 = (bf16[384,384]{1,0:T(8,128)(2,1)}, bf16[384,384]{1,0:T(8,128)(2,1)S(1)}, u32[]{:S(2)}) copy-start(bf16[384,384]{1,0:T(8,128)(2,1)S(1)} %get-tuple-element.12.spread_ref) | copy-start | bytes 884740
  79.3 1.1 copy-start.2
  80.4 23.1 %all-to-all-start.1 = ((bf16[8,160,512]{2,1,0:T(8,128)(2,1)}), bf16[8,160,512]{2,1,0:T(8,128)(2,1)S(1)}, u32[]{:S(2)}, u32[]{:S(2)}) async-start(bf16[8,160,512]{2,1,0:T(8,128)(2,1)} %copy-done.2), calls=%async_computation.1 | async-start | bytes 2621440 | tf_op jit(solution)/shard_map/all_to_all | solution.py:213
  105.9 60.4 %copy-start.1 = (bf16[5,240,384]{2,1,0:T(8,128)(2,1)S(1)}, bf16[5,240,384]{2,1,0:T(8,128)(2,1)}, u32[]{:S(2)}) copy-start(bf16[5,240,384]{2,1,0:T(8,128)(2,1)} %ens_ref.3) | copy-start | bytes 2764804
  105.9 60.4 %copy-start.4 = (bf16[384,384]{1,0:T(8,128)(2,1)S(1)}, bf16[384,384]{1,0:T(8,128)(2,1)}, u32[]{:S(2)}) copy-start(bf16[384,384]{1,0:T(8,128)(2,1)} %copy-done.3) | copy-start | bytes 884740

commit v2 on v1

--- a/solution.py
+++ b/solution.py
@@ -20,6 +20,7 @@
 BF = jnp.bfloat16
 F32 = jnp.float32
 VMEM_BYTES = 40 * 1024 * 1024
+SOURCE_VMEM_BYTES = 60 * 1024 * 1024
 
 
 def iota(shape, dim):
@@ -42,7 +43,14 @@
     return [(half, m, group * 32 + half * 16) for half in range(2) for m in range(MEMBERS)]
 
 
-def source_kernel(mem_ref, ens_ref, margin_ref, owner_ref, patch_ref, letkf_ref, out_ref, spread_ref):
+def source_kernel(mem_ref, *refs):
+    sources, (out_ref, spread_ref), landed, sems = refs[:5], refs[5:7], refs[7:12], refs[12]
+    copies = [pltpu.make_async_copy(a, b, sems.at[k]) for k, (a, b) in enumerate(zip(sources, landed))]
+    for copy in copies:
+        copy.start()
+    for copy in copies[1:]:
+        copy.wait()
+    ens_ref, margin_ref, owner_ref, patch_ref, letkf_ref = landed
     lane24 = iota((24, ELEMENTS), 1)
     block_of = (lane24 // 128) * 8 + lane24 % 8
     pick_block = iota((24, ELEMENTS), 0) == block_of
@@ -82,6 +90,7 @@
         parts(place) + parts(high) + parts(low) + [jnp.zeros((7, 128), F32), weights], axis=0
     )
 
+    copies[0].wait()
     for group in range(8):
         tiles = []
         for half, m, start in member_tiles(group):
@@ -149,7 +158,7 @@
             for n in range(MEMBERS):
                 row = (half * MEMBERS + n) * 16
                 inc_ref[row : row + 16, at] = mixed[n] - own_ref[0, row : row + 16, at].astype(F32)
-    side = got_ref[...].reshape(MESH * ROWS, 128).astype(F32)
+    side = got_ref[:, :, 384:512].reshape(MESH * ROWS, 128).astype(F32)
     first = inc_ref[0:128, :].T.astype(BF)
     small = inc_ref[128:160, :]
     last = jnp.zeros((MESH * ROWS, 128), F32)
@@ -187,14 +196,14 @@
     return pl.BlockSpec(memory_space=pltpu.VMEM)
 
 
-def call(kernel, outs, ins, scratch=()):
+def call(kernel, outs, ins, scratch=(), limit=VMEM_BYTES):
     return pl.pallas_call(
         kernel,
         out_shape=[jax.ShapeDtypeStruct(s, d) for s, d in outs],
         in_specs=ins,
         out_specs=[vmem() for _ in outs],
         scratch_shapes=list(scratch),
-        compiler_params=pltpu.CompilerParams(vmem_limit_bytes=VMEM_BYTES),
+        compiler_params=pltpu.CompilerParams(vmem_limit_bytes=limit),
     )
 
 
@@ -204,7 +213,16 @@
     send, spread = call(
         source_kernel,
         [((MESH, ROWS, WIDTH), BF), ((ELEMENTS, ELEMENTS), BF)],
-        [pl.BlockSpec(memory_space=pltpu.SMEM)] + [vmem()] * 5,
+        [pl.BlockSpec(memory_space=pltpu.SMEM)] + [pl.BlockSpec(memory_space=pltpu.HBM)] * 5,
+        [
+            pltpu.VMEM((MEMBERS, CHANNELS, ELEMENTS), BF),
+            pltpu.VMEM((256, 24), BF),
+            pltpu.VMEM((2, 24), jnp.int32),
+            pltpu.VMEM((2, 24), jnp.int32),
+            pltpu.VMEM((MEM * MEMBERS, MEM * MEMBERS), F32),
+            pltpu.SemaphoreType.DMA((5,)),
+        ],
+        SOURCE_VMEM_BYTES,
     )(mem, ensemble, margin, ovl_owner.T, ovl_patch.T, letkf_weight[0])
     got = lax.all_to_all(send, "mesh", split_axis=0, concat_axis=0, tiled=True)
     copies, weight = call(
@@ -216,7 +234,7 @@
         [((MESH, ROWS, WIDTH), BF)],
         [vmem()] * 4,
         [pltpu.VMEM((COLUMNS, PATCHES), F32)],
-    )(grid, copies[0:1], weight, got[:, :, 384:512])
+    )(grid, copies, weight, got)
     returned = lax.all_to_all(back, "mesh", split_axis=0, concat_axis=0, tiled=True)
     (analysis,) = call(final_kernel, [((MEMBERS, CHANNELS, ELEMENTS), BF)], [vmem()] * 3)(
         returned, ensemble, spread

time: 169 us -> 166 us (0.982)
  blocking collectives: 133 us -> 156 us
  waiting for transfers between devices: 17.8 us -> 0 us
  local copies, waits for them, and re-layouts: 6.18 us -> 0.01 us
  starting transfers between devices: 4.3 us -> 0 us
  Pallas kernels: 7.23 us -> 9.46 us
    all_to_all x0 -> x1, blocking collectives: none -> 23 us  [shards(): lax.all_to_all(copies, 'mem', split_axis=0, concat_axis=0, tiled=True)]
    all_to_all x1 -> x0, waiting for transfers between devices: 17.8 us -> none  [shards(): lax.all_to_all(copies, 'mem', split_axis=0, concat_axis=0, tiled=True)]
    unnamed x18 -> x4, local copies, waits for them, and re-layouts: 5.2 us -> 0.01 us
    all_to_all x1 -> x0, starting transfers between devices: 4.3 us -> none  [shards(): lax.all_to_all(copies, 'mem', split_axis=0, concat_axis=0, tiled=True)]
    pallas_call x1, Pallas kernels: 1.36 us -> 3.59 us  [shards(): call(source_kernel, [((MESH, ROWS, WIDTH), BF), ((ELEMENTS, ELEMENTS), BF...]
  transfers between devices with their start and end apart: 1 -> 0, of which waited for: 1 -> 0; matrix products, arithmetic and copies ran while one was open for 1% -> 0% of each run, Pallas kernels for 0% -> 0%
where the time goes in v2:
time: 166 us; the launch traced here: 165 us
  blocking collectives  156 us (94%)
  Pallas kernels  9.46 us (6%)
    all_to_all x1, blocking collectives, shards(): got = lax.all_to_all(send, 'mesh', split_axis=0, concat_axis=0, tiled=True)  72.6 us
    all_to_all x1, blocking collectives, shards(): lax.all_to_all(back, 'mesh', split_axis=0, concat_axis=0, tiled=True)  60.2 us
    all_to_all x1, blocking collectives, shards(): lax.all_to_all(copies, 'mem', split_axis=0, concat_axis=0, tiled=True)  23 us
    pallas_call x1, Pallas kernels, shards(): call(source_kernel, [((MESH, ROWS, WIDTH), BF), ((ELEMENTS, ELEMENTS), BF...  3.59 us

profile of v2, /device:TPU:8, one launch (start us, length us, event | category | flops | bytes accessed | tf_op | source)
XLA Modules:
  0.0 165.3 jit_solution(1466590967631850248)
XLA Ops:
  0.0 3.6 %shard_map.55 = (bf16[64,16,512]{2,1,0:T(8,128)(2,1)}, bf16[384,384]{1,0:T(8,128)(2,1)}) custom-call(s32[1]{0:T(128)} %bitcast.mem_ref, bf16[5,240,384]{2,1,0:T(8,128)(2,1)} %ens_ref.1, bf16[256,24]{1,0:T(8,128)(2,1)} %bitcast.7, s32[2,24]{1,0:T(2,128)} %bitcast.9, s32[2,24]{1,0:T(2,128)} %bitcast.10, f32[40,40]{1,0:T(8,128)} %bitcast.8), custom_call_target="tpu_custom_call" | custom-call | tf_op jit(solution)/shard_map/pallas_call | solution.py:213
  3.6 72.6 %all_to_all.15.got_ref = bf16[64,16,512]{2,1,0:T(8,128)(2,1)S(1)} all-to-all(bf16[64,16,512]{2,1,0:T(8,128)(2,1)} %get-tuple-element.9), channel_id=1, replica_groups=mesh['mesh'=64,'mem'=8] {'mesh'}, dimensions={0} | all-to-all | bytes 2097152 | tf_op jit(solution)/shard_map/all_to_all | solution.py:227
  76.2 1.5 shard_map.56
  77.6 23.0 %all_to_all.16.grid_ref = bf16[8,160,512]{2,1,0:T(8,128)(2,1)S(1)} all-to-all(bf16[8,160,512]{2,1,0:T(8,128)(2,1)S(1)} %get-tuple-element.10.own_ref), channel_id=1, replica_groups=mesh['mesh'=64,'mem'=8] {'mem'}, dimensions={0} | all-to-all | bytes 2621440 | tf_op jit(solution)/shard_map/all_to_all | solution.py:231
  100.7 2.4 %shard_map.57 = bf16[64,16,512]{2,1,0:T(8,128)(2,1)S(1)} custom-call(bf16[8,160,512]{2,1,0:T(8,128)(2,1)S(1)} %all_to_all.16.grid_ref, bf16[8,160,512]{2,1,0:T(8,128)(2,1)S(1)} %get-tuple-element.10.own_ref, f32[256,512]{1,0:T(8,128)S(1)} %get-tuple-element.11.weight_ref, bf16[64,16,512]{2,1,0:T(8,128)(2,1)S(1)} %all_to_all.15.got_ref), custom_call_target="tpu_custom_call" | custom-call | tf_op jit(solution)/shard_map/pallas_call | solution.py:232
  103.1 0.0 copy-start
  103.1 0.0 copy-start.1
  103.1 60.2 %all_to_all.17.back_ref = bf16[64,16,512]{2,1,0:T(8,128)(2,1)S(1)} all-to-all(bf16[64,16,512]{2,1,0:T(8,128)(2,1)S(1)} %shard_map.57), channel_id=1, replica_groups=mesh['mesh'=64,'mem'=8] {'mesh'}, dimensions={0} | all-to-all | bytes 2097152 | tf_op jit(solution)/shard_map/all_to_all | solution.py:238
  163.3 0.0 copy-done
  163.3 0.0 copy-done.1
  163.3 2.0 %shard_map.58 = bf16[5,240,384]{2,1,0:T(8,128)(2,1)} custom-call(bf16[64,16,512]{2,1,0:T(8,128)(2,1)S(1)} %all_to_all.17.back_ref, bf16[5,240,384]{2,1,0:T(8,128)(2,1)S(1)} %copy-done, bf16[384,384]{1,0:T(8,128)(2,1)S(1)} %copy-done.1), custom_call_target="tpu_custom_call" | custom-call | tf_op jit(solution)/shard_map/pallas_call | solution.py:239
Async XLA Ops:
  103.1 60.2 %copy-start = (bf16[5,240,384]{2,1,0:T(8,128)(2,1)S(1)}, bf16[5,240,384]{2,1,0:T(8,128)(2,1)}, u32[]{:S(2)}) copy-start(bf16[5,240,384]{2,1,0:T(8,128)(2,1)} %ens_ref.1) | copy-start | bytes 2764804
  103.1 60.2 %copy-start.1 = (bf16[384,384]{1,0:T(8,128)(2,1)S(1)}, bf16[384,384]{1,0:T(8,128)(2,1)}, u32[]{:S(2)}) copy-start(bf16[384,384]{1,0:T(8,128)(2,1)} %get-tuple-element.12.spread_ref) | copy-start | bytes 884740

commit v3 on v2

--- a/solution.py
+++ b/solution.py
@@ -16,7 +16,6 @@
 THIRDS = 3
 WIDTH = 512
 SIDE = 96
-COLUMNS = 160
 BF = jnp.bfloat16
 F32 = jnp.float32
 VMEM_BYTES = 40 * 1024 * 1024
@@ -112,7 +111,7 @@
     return one_hot(lanes == place)
 
 
-def patch_kernel(got_ref, out_ref, weight_ref):
+def patch_kernel(got_ref, out_ref):
     got = got_ref[...].reshape(MESH * ROWS, WIDTH)
     last = got[:, 384:512].astype(F32)
     last_t = last.T.astype(BF)
@@ -127,40 +126,47 @@
         rest = rest + sums[128:160]
         cover = cover + sums[163 + h : 164 + h] + sums[166 + h : 167 + h]
     cover = jnp.maximum(cover, 1.0)
-    total = (total / cover).astype(BF)
-    rest = (rest / cover).astype(BF)
+    grid = jnp.concatenate([total, rest], axis=0) / cover
     for q in range(MEM):
-        out_ref[q, 0:128, :] = total
-        out_ref[q, 128:160, :] = rest
-
-    wide = last_t[112:128]
-    lane = iota((ROWS, MESH * ROWS), 1)
-    rows = jnp.concatenate(
-        [jnp.where(lane % 16 == r, wide, jnp.zeros_like(wide)) for r in range(ROWS)], axis=0
-    )
-    tile = one_hot(
-        iota((MESH * ROWS, PATCHES), 0) // 16 == iota((MESH * ROWS, PATCHES), 1) // 8
-    )
-    weight_ref[...] = dot(rows, tile)
-
-
-def mixing_kernel(grid_ref, own_ref, weight_ref, got_ref, out_ref, inc_ref):
-    for half in range(2):
-        for lanes in range(PATCHES // 128):
-            at = slice(128 * lanes, 128 * lanes + 128)
-            mixed = [jnp.zeros((16, 128), F32) for _ in range(MEMBERS)]
-            for m in range(MEM * MEMBERS):
-                row = (half * MEMBERS + m % MEMBERS) * 16
-                field = grid_ref[m // MEMBERS, row : row + 16, at].astype(F32)
-                for n in range(MEMBERS):
-                    w = (m % 16) * 16 + n * 3 + m // 16
-                    mixed[n] = mixed[n] + weight_ref[w : w + 1, at] * field
+        at = slice(64 * q, 64 * q + 64)
+        out_ref[q, 0:80, :] = jnp.concatenate([grid[0:80, at], grid[80:160, at]], axis=1).astype(BF)
+        out_ref[q, 80:96, :] = last_t[112:128, 128 * q : 128 * q + 128]
+
+
+def mixing_kernel(got_ref, out_ref, weight_ref, field_ref):
+    tile = one_hot(iota((128, 128), 0) // 16 == (iota((128, 128), 1) % 64) // 8)
+    lane = iota((ROWS, 128), 1)
+    for q in range(MEM):
+        wide = got_ref[q, 80:96, :]
+        rows = [jnp.where(lane % 16 == r, wide, jnp.zeros_like(wide)) for r in range(ROWS)]
+        weight_ref[q] = dot(jnp.concatenate(rows, axis=0), tile)
+        field_ref[q] = got_ref[q, 0:80, :].astype(F32)
+
+    def mix(q, carry):
+        mixed = [jnp.zeros((16, 128), F32) for _ in range(MEMBERS)]
+        for m in range(MEM * MEMBERS):
+            row = (m % MEMBERS) * 16
+            field = field_ref[m // MEMBERS, row : row + 16, :]
             for n in range(MEMBERS):
-                row = (half * MEMBERS + n) * 16
-                inc_ref[row : row + 16, at] = mixed[n] - own_ref[0, row : row + 16, at].astype(F32)
+                w = (m % 16) * 16 + n * 3 + m // 16
+                mixed[n] = mixed[n] + weight_ref[q, w : w + 1, :] * field
+        for n in range(MEMBERS):
+            out_ref[q, 16 * n : 16 * n + 16, :] = (mixed[n] - field_ref[q, 16 * n : 16 * n + 16, :]).astype(BF)
+        return carry
+
+    lax.fori_loop(0, MEM, mix, 0)
+
+
+def expand_kernel(inc_ref, got_ref, out_ref):
+    halves = [[], []]
+    for q in range(0, MEM, 2):
+        even, odd = inc_ref[q].astype(F32), inc_ref[q + 1].astype(F32)
+        halves[0].append(jnp.concatenate([even[:, 0:64], odd[:, 0:64]], axis=1))
+        halves[1].append(jnp.concatenate([even[:, 64:128], odd[:, 64:128]], axis=1))
+    inc = jnp.concatenate([jnp.concatenate(half, axis=1) for half in halves], axis=0)
     side = got_ref[:, :, 384:512].reshape(MESH * ROWS, 128).astype(F32)
-    first = inc_ref[0:128, :].T.astype(BF)
-    small = inc_ref[128:160, :]
+    first = inc[0:128].T.astype(BF)
+    small = inc[128:160]
     last = jnp.zeros((MESH * ROWS, 128), F32)
     for h in range(THIRDS):
         pad = [jnp.zeros((32, PATCHES), F32)] * 4
@@ -225,16 +231,16 @@
         SOURCE_VMEM_BYTES,
     )(mem, ensemble, margin, ovl_owner.T, ovl_patch.T, letkf_weight[0])
     got = lax.all_to_all(send, "mesh", split_axis=0, concat_axis=0, tiled=True)
-    copies, weight = call(
-        patch_kernel, [((MEM, COLUMNS, PATCHES), BF), ((256, PATCHES), F32)], [vmem()]
-    )(got)
-    grid = lax.all_to_all(copies, "mem", split_axis=0, concat_axis=0, tiled=True)
-    (back,) = call(
+    (fields,) = call(patch_kernel, [((MEM, 96, 128), BF)], [vmem()])(got)
+    fields = lax.all_to_all(fields, "mem", split_axis=0, concat_axis=0, tiled=True)
+    (mixed,) = call(
         mixing_kernel,
-        [((MESH, ROWS, WIDTH), BF)],
-        [vmem()] * 4,
-        [pltpu.VMEM((COLUMNS, PATCHES), F32)],
-    )(grid, copies, weight, got)
+        [((MEM, 80, 128), BF)],
+        [vmem()],
+        [pltpu.VMEM((MEM, 256, 128), F32), pltpu.VMEM((MEM, 80, 128), F32)],
+    )(fields)
+    mixed = lax.all_to_all(mixed, "mem", split_axis=0, concat_axis=0, tiled=True)
+    (back,) = call(expand_kernel, [((MESH, ROWS, WIDTH), BF)], [vmem()] * 2)(mixed, got)
     returned = lax.all_to_all(back, "mesh", split_axis=0, concat_axis=0, tiled=True)
     (analysis,) = call(final_kernel, [((MEMBERS, CHANNELS, ELEMENTS), BF)], [vmem()] * 3)(
         returned, ensemble, spread

time: 166 us -> 163 us (0.982)
  blocking collectives: 156 us -> 153 us
    all_to_all x1 -> x2, blocking collectives: 23 us -> 19.8 us  [the longest x1 10.9 us: shards(): lax.all_to_all(fields, 'mem', split_axis=0, concat_axis=0, tiled=True)]
    pallas_call x2 -> x3, Pallas kernels: 3.9 us -> 4 us  [the longest x1 1.42 us: shards(): call(mixing_kernel, [((MEM, 80, 128), BF)], [vmem()], [pltpu.VMEM((MEM, 2...]
where the time goes in v3:
time: 163 us; the launch traced here: 162 us
  blocking collectives  153 us (94%)
  Pallas kernels  9.58 us (6%)
    all_to_all x1, blocking collectives, shards(): got = lax.all_to_all(send, 'mesh', split_axis=0, concat_axis=0, tiled=True)  72.6 us
    all_to_all x1, blocking collectives, shards(): lax.all_to_all(back, 'mesh', split_axis=0, concat_axis=0, tiled=True)  60.3 us
    all_to_all x1, blocking collectives, shards(): lax.all_to_all(fields, 'mem', split_axis=0, concat_axis=0, tiled=True)  10.9 us
    all_to_all x1, blocking collectives, shards(): lax.all_to_all(mixed, 'mem', split_axis=0, concat_axis=0, tiled=True)  8.88 us
    pallas_call x1, Pallas kernels, shards(): call(source_kernel, [((MESH, ROWS, WIDTH), BF), ((ELEMENTS, ELEMENTS), BF...  3.59 us

profile of v3, /device:TPU:8, one launch (start us, length us, event | category | flops | bytes accessed | tf_op | source)
XLA Modules:
  0.0 162.3 jit_solution(5993793383190352703)
XLA Ops:
  0.0 3.6 %shard_map.55 = (bf16[64,16,512]{2,1,0:T(8,128)(2,1)}, bf16[384,384]{1,0:T(8,128)(2,1)}) custom-call(s32[1]{0:T(128)} %bitcast.mem_ref, bf16[5,240,384]{2,1,0:T(8,128)(2,1)} %ens_ref.1, bf16[256,24]{1,0:T(8,128)(2,1)} %bitcast.7, s32[2,24]{1,0:T(2,128)} %bitcast.9, s32[2,24]{1,0:T(2,128)} %bitcast.10, f32[40,40]{1,0:T(8,128)} %bitcast.8), custom_call_target="tpu_custom_call" | custom-call | tf_op jit(solution)/shard_map/pallas_call | solution.py:219
  3.6 72.6 %all_to_all.20.got_ref = bf16[64,16,512]{2,1,0:T(8,128)(2,1)S(1)} all-to-all(bf16[64,16,512]{2,1,0:T(8,128)(2,1)} %get-tuple-element.7), channel_id=1, replica_groups=mesh['mesh'=64,'mem'=8] {'mesh'}, dimensions={0} | all-to-all | bytes 2097152 | tf_op jit(solution)/shard_map/all_to_all | solution.py:233
  76.2 1.2 shard_map.56
  77.4 10.9 %all_to_all.21.got_ref = bf16[8,96,128]{2,1,0:T(8,128)(2,1)S(1)} all-to-all(bf16[8,96,128]{2,1,0:T(8,128)(2,1)S(1)} %shard_map.56), channel_id=1, replica_groups=mesh['mesh'=64,'mem'=8] {'mem'}, dimensions={0} | all-to-all | bytes 393216 | tf_op jit(solution)/shard_map/all_to_all | solution.py:235
  88.3 1.4 shard_map.57
  89.7 8.9 %all_to_all.22.inc_ref = bf16[8,80,128]{2,1,0:T(8,128)(2,1)S(1)} all-to-all(bf16[8,80,128]{2,1,0:T(8,128)(2,1)S(1)} %shard_map.57), channel_id=1, replica_groups=mesh['mesh'=64,'mem'=8] {'mem'}, dimensions={0} | all-to-all | bytes 327680 | tf_op jit(solution)/shard_map/all_to_all | solution.py:242
  98.6 1.4 shard_map.58
  100.0 0.0 copy-start
  100.0 0.0 copy-start.1
  100.0 60.3 %all_to_all.23.back_ref = bf16[64,16,512]{2,1,0:T(8,128)(2,1)S(1)} all-to-all(bf16[64,16,512]{2,1,0:T(8,128)(2,1)S(1)} %shard_map.58), channel_id=1, replica_groups=mesh['mesh'=64,'mem'=8] {'mesh'}, dimensions={0} | all-to-all | bytes 2097152 | tf_op jit(solution)/shard_map/all_to_all | solution.py:244
  160.3 0.0 copy-done
  160.3 0.0 copy-done.1
  160.3 2.0 %shard_map.59 = bf16[5,240,384]{2,1,0:T(8,128)(2,1)} custom-call(bf16[64,16,512]{2,1,0:T(8,128)(2,1)S(1)} %all_to_all.23.back_ref, bf16[5,240,384]{2,1,0:T(8,128)(2,1)S(1)} %copy-done, bf16[384,384]{1,0:T(8,128)(2,1)S(1)} %copy-done.1), custom_call_target="tpu_custom_call" | custom-call | tf_op jit(solution)/shard_map/pallas_call | solution.py:245
Async XLA Ops:
  100.0 60.3 %copy-start = (bf16[5,240,384]{2,1,0:T(8,128)(2,1)S(1)}, bf16[5,240,384]{2,1,0:T(8,128)(2,1)}, u32[]{:S(2)}) copy-start(bf16[5,240,384]{2,1,0:T(8,128)(2,1)} %ens_ref.1) | copy-start | bytes 2764804
  100.0 60.3 %copy-start.1 = (bf16[384,384]{1,0:T(8,128)(2,1)S(1)}, bf16[384,384]{1,0:T(8,128)(2,1)}, u32[]{:S(2)}) copy-start(bf16[384,384]{1,0:T(8,128)(2,1)} %get-tuple-element.8.spread_ref) | copy-start | bytes 884740

commit v4 on v3

--- a/solution.py
+++ b/solution.py
@@ -14,8 +14,9 @@
 PATCHES = 512
 ROWS = 16
 THIRDS = 3
-WIDTH = 512
-SIDE = 96
+QUARTERS = 4
+WIDTH = 1920
+WIDE_ROWS = 1216
 BF = jnp.bfloat16
 F32 = jnp.float32
 VMEM_BYTES = 40 * 1024 * 1024
@@ -38,12 +39,55 @@
     return jnp.where(mask, 1.0, 0.0).astype(BF)
 
 
-def member_tiles(group):
-    return [(half, m, group * 32 + half * 16) for half in range(2) for m in range(MEMBERS)]
+def turn(value, shift):
+    return pltpu.roll(value, shift, 2)
+
+
+def pack(out_ref, at, firsts, last):
+    for h in range(THIRDS):
+        block = firsts[h]
+        for a in range(QUARTERS):
+            lanes = slice(128 * (3 * a + h), 128 * (3 * a + h) + 128)
+            out_ref[at, :, lanes] = block[:, 4 * a : 4 * a + 4, :].astype(BF)
+    n = last.shape[0]
+    front = iota((n, 4, 128), 2) < 96
+    for i in range(THIRDS):
+        tail = turn(last, 96 - 32 * i)[:, 12:16, :]
+        lanes = slice(128 * (12 + i), 128 * (12 + i) + 128)
+        out_ref[at, :, lanes] = jnp.where(front, last[:, 4 * i : 4 * i + 4, :], tail).astype(BF)
+
+
+def unpack(ref, at, h):
+    parts = []
+    for a in range(QUARTERS):
+        lanes = slice(128 * (3 * a + h), 128 * (3 * a + h) + 128)
+        parts.append(ref[at, :, lanes].astype(F32))
+    return jnp.concatenate(parts, axis=1)
+
+
+def unpack_last(ref, at):
+    tiles = [ref[at, :, 128 * (12 + i) : 128 * (12 + i) + 128].astype(F32) for i in range(THIRDS)]
+    lane = iota(tiles[0].shape, 2) // 32
+    tail = turn(tiles[0], 32)
+    for h in range(1, THIRDS):
+        tail = jnp.where(lane == h, turn(tiles[h], 32 * h + 32), tail)
+    return jnp.concatenate(tiles + [tail], axis=1)
+
+
+def places(group):
+    return [m * CHANNELS + 2 * group + parity for parity in range(2) for m in range(MEMBERS)]
+
+
+def widen(ens_ref, wide_ref):
+    for m in range(MEMBERS):
+        for j in range(3):
+            rows = slice(m * CHANNELS, (m + 1) * CHANNELS)
+            wide_ref[j, rows, :] = ens_ref[m, :, 128 * j : 128 * j + 128].astype(F32)
 
 
 def source_kernel(mem_ref, *refs):
     sources, (out_ref, spread_ref), landed, sems = refs[:5], refs[5:7], refs[7:12], refs[12]
+    wide_ref = refs[13]
     copies = [pltpu.make_async_copy(a, b, sems.at[k]) for k, (a, b) in enumerate(zip(sources, landed))]
     for copy in copies:
         copy.start()
@@ -76,61 +120,57 @@
     place = jnp.sum(jnp.where((lane2 % 16) // 8 == iota((2, ELEMENTS), 0), place, 0.0), axis=0, keepdims=True)
 
     own = mem_ref[0] * MEMBERS
-    pick_own = one_hot((iota((16, 40), 1) == own + iota((16, 40), 0) // 3) & (iota((16, 40), 0) < 15))
-    mine = dot_nt(pick_own, letkf_ref[...].astype(BF))
-    keep = (iota((16, 40), 1) // 16) == iota((16, 40), 0) % 3
-    mine = jnp.where(keep, mine, 0.0).astype(BF)
-    weights = dot(mine, one_hot(iota((40, 128), 0) % 16 == iota((40, 128), 1) % 16))
-
-    def parts(value):
-        return [value[:, 128 * h : 128 * h + 128] for h in range(THIRDS)]
-
-    side = jnp.concatenate(
-        parts(place) + parts(high) + parts(low) + [jnp.zeros((7, 128), F32), weights], axis=0
-    )
+    pick_own = one_hot((iota((16, 40), 1) == own + iota((16, 40), 0)) & (iota((16, 40), 0) < MEMBERS))
+    mine = dot_nt(pick_own, letkf_ref[...].astype(BF)).astype(BF)
+    lane40 = iota((40, ELEMENTS), 1)
+    weights = dot(mine, one_hot(iota((40, ELEMENTS), 0) == (lane40 // 128) * 16 + lane40 % 16))
+    sides = [place, high, low] + [weights[n : n + 1] for n in range(MEMBERS)] + [jnp.zeros_like(low)] * 2
+    spare = iota((16, ELEMENTS), 0) == 15
 
     copies[0].wait()
+    widen(ens_ref, wide_ref)
     for group in range(8):
-        tiles = []
-        for half, m, start in member_tiles(group):
-            if start < CHANNELS:
-                tiles.append(ens_ref[m, start : start + 16, :])
-            else:
-                tiles.append(jnp.zeros((16, ELEMENTS), BF))
-        pieces = dot(jnp.concatenate(tiles, axis=0), spread)
-        for h in range(THIRDS):
-            block = pieces[0:128, 128 * h : 128 * h + 128].T.astype(BF)
-            out_ref[8 * group : 8 * group + 8, :, 128 * h : 128 * h + 128] = block.reshape(8, ROWS, 128)
-        rest = jnp.concatenate(parts(pieces[128:160]) + [side], axis=0)
-        out_ref[8 * group : 8 * group + 8, :, 384:512] = rest.T.astype(BF).reshape(8, ROWS, 128)
-
-
-def hits(side, h):
-    place = side[:, SIDE + h : SIDE + h + 1].astype(F32) + 256.0
+        tiles = [
+            jnp.concatenate([wide_ref[j, pl.ds(start, 16, 16), :] for j in range(3)], axis=1)
+            for start in places(group)
+        ]
+        pieces = dot(jnp.concatenate(tiles, axis=0).astype(BF), spread)
+        pieces = jnp.concatenate(
+            [jnp.where(spare, sides[k], pieces[16 * k : 16 * k + 16]) for k in range(10)], axis=0
+        )
+        firsts = [pieces[0:128, 128 * h : 128 * h + 128].T.reshape(8, ROWS, 128) for h in range(THIRDS)]
+        rest = [pieces[128:160, 128 * h : 128 * h + 128] for h in range(THIRDS)]
+        rest = jnp.concatenate(rest + [jnp.zeros((32, 128), F32)], axis=0)
+        pack(out_ref, slice(8 * group, 8 * group + 8), firsts, rest.T.reshape(8, ROWS, 128))
+
+
+def hits(first):
+    place = first[:, 15:16] + 256.0
     lanes = iota((MESH * ROWS, PATCHES), 1).astype(F32)
     return one_hot(lanes == place)
 
 
 def patch_kernel(got_ref, out_ref):
-    got = got_ref[...].reshape(MESH * ROWS, WIDTH)
-    last = got[:, 384:512].astype(F32)
-    last_t = last.T.astype(BF)
-    total = jnp.zeros((128, PATCHES), F32)
-    rest = jnp.zeros((32, PATCHES), F32)
-    cover = jnp.zeros((1, PATCHES), F32)
+    every = slice(0, MESH)
+    last_t = unpack_last(got_ref, every).reshape(MESH * ROWS, 128).T
+    grid = jnp.zeros((160, PATCHES), F32)
+    weights = [[None] * THIRDS for _ in range(MEMBERS)]
     for h in range(THIRDS):
-        first_t = got[:, 128 * h : 128 * h + 128].astype(F32).T.astype(BF)
-        left = jnp.concatenate([first_t, last_t[32 * h : 32 * h + 32], last_t[96:112]], axis=0)
-        sums = dot(left, hits(last, h))
-        total = total + sums[0:128]
-        rest = rest + sums[128:160]
-        cover = cover + sums[163 + h : 164 + h] + sums[166 + h : 167 + h]
+        first = unpack(got_ref, every, h).reshape(MESH * ROWS, 128)
+        first_t = first.T
+        left = jnp.concatenate([first_t, last_t[32 * h : 32 * h + 32]], axis=0).astype(BF)
+        grid = grid + dot(left, hits(first))
+        for n in range(MEMBERS):
+            weights[n][h] = first_t[63 + 16 * n : 64 + 16 * n]
+    cover = grid[31:32] + grid[47:48]
+    weights = sum(weights, []) + [jnp.zeros((1, MESH * ROWS), F32)]
+    weights = jnp.concatenate(weights, axis=0).astype(BF)
     cover = jnp.maximum(cover, 1.0)
-    grid = jnp.concatenate([total, rest], axis=0) / cover
+    grid = grid / cover
     for q in range(MEM):
         at = slice(64 * q, 64 * q + 64)
         out_ref[q, 0:80, :] = jnp.concatenate([grid[0:80, at], grid[80:160, at]], axis=1).astype(BF)
-        out_ref[q, 80:96, :] = last_t[112:128, 128 * q : 128 * q + 128]
+        out_ref[q, 80:96, :] = weights[:, 128 * q : 128 * q + 128]
 
 
 def mixing_kernel(got_ref, out_ref, weight_ref, field_ref):
@@ -164,38 +204,42 @@
         halves[0].append(jnp.concatenate([even[:, 0:64], odd[:, 0:64]], axis=1))
         halves[1].append(jnp.concatenate([even[:, 64:128], odd[:, 64:128]], axis=1))
     inc = jnp.concatenate([jnp.concatenate(half, axis=1) for half in halves], axis=0)
-    side = got_ref[:, :, 384:512].reshape(MESH * ROWS, 128).astype(F32)
     first = inc[0:128].T.astype(BF)
     small = inc[128:160]
     last = jnp.zeros((MESH * ROWS, 128), F32)
+    every = slice(0, MESH)
+    firsts = []
     for h in range(THIRDS):
         pad = [jnp.zeros((32, PATCHES), F32)] * 4
         pad[h] = small
         right = jnp.concatenate([first, jnp.concatenate(pad, axis=0).T.astype(BF)], axis=1)
-        back = dot(hits(side, h), right)
-        out_ref[:, :, 128 * h : 128 * h + 128] = back[:, 0:128].astype(BF).reshape(MESH, ROWS, 128)
+        back = dot(hits(unpack(got_ref, every, h).reshape(MESH * ROWS, 128)), right)
+        firsts.append(back[:, 0:128].reshape(MESH, ROWS, 128))
         last = last + back[:, 128:256]
-    out_ref[:, :, 384:512] = last.astype(BF).reshape(MESH, ROWS, 128)
-
-
-def final_kernel(back_ref, ens_ref, spread_ref, out_ref):
+    pack(out_ref, every, firsts, last.reshape(MESH, ROWS, 128))
+
+
+def final_kernel(back_ref, ens_ref, spread_ref, out_ref, wide_ref):
     spread = spread_ref[...]
     area = dot_nt(jnp.ones((16, ELEMENTS), BF), spread)[0:1]
     scale = 1.0 / area
+    widen(ens_ref, wide_ref)
     for group in range(8):
-        def turned(k):
-            block = back_ref[8 * group : 8 * group + 8, :, 128 * k : 128 * k + 128]
-            return block.reshape(128, 128).astype(F32).T
-
-        first = jnp.concatenate([turned(h) for h in range(THIRDS)], axis=1)
-        last = turned(3)
+        at = slice(8 * group, 8 * group + 8)
+        first = jnp.concatenate([unpack(back_ref, at, h).reshape(128, 128).T for h in range(THIRDS)], axis=1)
+        last = unpack_last(back_ref, at).reshape(128, 128).T
         last = jnp.concatenate([last[32 * h : 32 * h + 32] for h in range(THIRDS)], axis=1)
         left = jnp.concatenate([first, last], axis=0).astype(BF)
         correction = dot_nt(left, spread) * scale
-        for k, (half, m, start) in enumerate(member_tiles(group)):
-            if start < CHANNELS:
-                value = ens_ref[m, start : start + 16, :].astype(F32) + correction[16 * k : 16 * k + 16]
-                out_ref[m, start : start + 16, :] = value.astype(BF)
+        for k, start in enumerate(places(group)):
+            rows = pl.ds(start, 15, 16)
+            for j in range(3):
+                change = correction[16 * k : 16 * k + 15, 128 * j : 128 * j + 128]
+                wide_ref[j, rows, :] = wide_ref[j, rows, :] + change
+    for m in range(MEMBERS):
+        for j in range(3):
+            rows = slice(m * CHANNELS, (m + 1) * CHANNELS)
+            out_ref[m, :, 128 * j : 128 * j + 128] = wide_ref[j, rows, :].astype(BF)
 
 
 def vmem():
@@ -218,7 +262,7 @@
     mem = lax.axis_index("mem").astype(jnp.int32).reshape(1)
     send, spread = call(
         source_kernel,
-        [((MESH, ROWS, WIDTH), BF), ((ELEMENTS, ELEMENTS), BF)],
+        [((MESH, QUARTERS, WIDTH), BF), ((ELEMENTS, ELEMENTS), BF)],
         [pl.BlockSpec(memory_space=pltpu.SMEM)] + [pl.BlockSpec(memory_space=pltpu.HBM)] * 5,
         [
             pltpu.VMEM((MEMBERS, CHANNELS, ELEMENTS), BF),
@@ -227,6 +271,7 @@
             pltpu.VMEM((2, 24), jnp.int32),
             pltpu.VMEM((MEM * MEMBERS, MEM * MEMBERS), F32),
             pltpu.SemaphoreType.DMA((5,)),
+            pltpu.VMEM((3, WIDE_ROWS, 128), F32),
         ],
         SOURCE_VMEM_BYTES,
     )(mem, ensemble, margin, ovl_owner.T, ovl_patch.T, letkf_weight[0])
@@ -240,11 +285,14 @@
         [pltpu.VMEM((MEM, 256, 128), F32), pltpu.VMEM((MEM, 80, 128), F32)],
     )(fields)
     mixed = lax.all_to_all(mixed, "mem", split_axis=0, concat_axis=0, tiled=True)
-    (back,) = call(expand_kernel, [((MESH, ROWS, WIDTH), BF)], [vmem()] * 2)(mixed, got)
+    (back,) = call(expand_kernel, [((MESH, QUARTERS, WIDTH), BF)], [vmem()] * 2)(mixed, got)
     returned = lax.all_to_all(back, "mesh", split_axis=0, concat_axis=0, tiled=True)
-    (analysis,) = call(final_kernel, [((MEMBERS, CHANNELS, ELEMENTS), BF)], [vmem()] * 3)(
-        returned, ensemble, spread
-    )
+    (analysis,) = call(
+        final_kernel,
+        [((MEMBERS, CHANNELS, ELEMENTS), BF)],
+        [vmem()] * 3,
+        [pltpu.VMEM((3, WIDE_ROWS, 128), F32)],
+    )(returned, ensemble, spread)
     return analysis
 
 

time: 163 us -> 160 us (0.982)
  blocking collectives: 153 us -> 147 us
  Pallas kernels: 9.58 us -> 12 us
    all_to_all x1, blocking collectives: 72.6 us -> 69.8 us  [shards(): got = lax.all_to_all(send, 'mesh', split_axis=0, concat_axis=0, tiled=True)]
    all_to_all x1, blocking collectives: 60.3 us -> 57.5 us  [shards(): lax.all_to_all(back, 'mesh', split_axis=0, concat_axis=0, tiled=True)]
    pallas_call x3, Pallas kernels: 6.94 us -> 9.2 us  [the longest x1 4.44 us: shards(): call(source_kernel, [((MESH, QUARTERS, WIDTH), BF), ((ELEMENTS, ELEMENTS)...]
where the time goes in v4:
time: 160 us; the launch traced here: 159 us
  blocking collectives  147 us (92%)
  Pallas kernels  12 us (8%)
    all_to_all x1, blocking collectives, shards(): got = lax.all_to_all(send, 'mesh', split_axis=0, concat_axis=0, tiled=True)  69.8 us
    all_to_all x1, blocking collectives, shards(): lax.all_to_all(back, 'mesh', split_axis=0, concat_axis=0, tiled=True)  57.5 us
    all_to_all x1, blocking collectives, shards(): lax.all_to_all(fields, 'mem', split_axis=0, concat_axis=0, tiled=True)  10.9 us
    all_to_all x1, blocking collectives, shards(): lax.all_to_all(mixed, 'mem', split_axis=0, concat_axis=0, tiled=True)  8.88 us
    pallas_call x1, Pallas kernels, shards(): call(source_kernel, [((MESH, QUARTERS, WIDTH), BF), ((ELEMENTS, ELEMENTS)...  4.44 us
    pallas_call x1, Pallas kernels, shards(): call(final_kernel, [((MEMBERS, CHANNELS, ELEMENTS), BF)], [vmem()] * 3, [...  3.39 us

profile of v4, /device:TPU:8, one launch (start us, length us, event | category | flops | bytes accessed | tf_op | source)
XLA Modules:
  0.0 159.2 jit_solution(15848006909838052453)
XLA Ops:
  0.0 4.4 %shard_map.55 = (bf16[64,4,1920]{2,1,0:T(4,128)(2,1)}, bf16[384,384]{1,0:T(8,128)(2,1)}) custom-call(s32[1]{0:T(128)} %bitcast.mem_ref, bf16[5,240,384]{2,1,0:T(8,128)(2,1)} %ens_ref.1, bf16[256,24]{1,0:T(8,128)(2,1)} %bitcast.7, s32[2,24]{1,0:T(2,128)} %bitcast.9, s32[2,24]{1,0:T(2,128)} %bitcast.10, f32[40,40]{1,0:T(8,128)} %bitcast.8), custom_call_target="tpu_custom_call" | custom-call | tf_op jit(solution)/shard_map/pallas_call | solution.py:263
  4.4 69.8 %all_to_all.20.got_ref = bf16[64,4,1920]{2,1,0:T(4,128)(2,1)S(1)} all-to-all(bf16[64,4,1920]{2,1,0:T(4,128)(2,1)} %get-tuple-element.7), channel_id=1, replica_groups=mesh['mesh'=64,'mem'=8] {'mesh'}, dimensions={0} | all-to-all | bytes 1966080 | tf_op jit(solution)/shard_map/all_to_all | solution.py:278
  74.2 1.4 shard_map.56
  75.7 10.9 %all_to_all.21.got_ref = bf16[8,96,128]{2,1,0:T(8,128)(2,1)S(1)} all-to-all(bf16[8,96,128]{2,1,0:T(8,128)(2,1)S(1)} %shard_map.56), channel_id=1, replica_groups=mesh['mesh'=64,'mem'=8] {'mem'}, dimensions={0} | all-to-all | bytes 393216 | tf_op jit(solution)/shard_map/all_to_all | solution.py:280
  86.6 1.4 shard_map.57
  88.0 8.9 %all_to_all.22.inc_ref = bf16[8,80,128]{2,1,0:T(8,128)(2,1)S(1)} all-to-all(bf16[8,80,128]{2,1,0:T(8,128)(2,1)S(1)} %shard_map.57), channel_id=1, replica_groups=mesh['mesh'=64,'mem'=8] {'mem'}, dimensions={0} | all-to-all | bytes 327680 | tf_op jit(solution)/shard_map/all_to_all | solution.py:287
  96.9 1.4 shard_map.58
  98.2 0.0 copy-start
  98.3 0.0 copy-start.1
  98.3 57.5 %all_to_all.23.back_ref = bf16[64,4,1920]{2,1,0:T(4,128)(2,1)S(1)} all-to-all(bf16[64,4,1920]{2,1,0:T(4,128)(2,1)S(1)} %shard_map.58), channel_id=1, replica_groups=mesh['mesh'=64,'mem'=8] {'mesh'}, dimensions={0} | all-to-all | bytes 1966080 | tf_op jit(solution)/shard_map/all_to_all | solution.py:289
  155.8 0.0 copy-done
  155.8 0.0 copy-done.1
  155.8 3.4 %shard_map.59 = bf16[5,240,384]{2,1,0:T(8,128)(2,1)} custom-call(bf16[64,4,1920]{2,1,0:T(4,128)(2,1)S(1)} %all_to_all.23.back_ref, bf16[5,240,384]{2,1,0:T(8,128)(2,1)S(1)} %copy-done, bf16[384,384]{1,0:T(8,128)(2,1)S(1)} %copy-done.1), custom_call_target="tpu_custom_call" | custom-call | tf_op jit(solution)/shard_map/pallas_call | solution.py:290
Async XLA Ops:
  98.2 57.6 %copy-start = (bf16[5,240,384]{2,1,0:T(8,128)(2,1)S(1)}, bf16[5,240,384]{2,1,0:T(8,128)(2,1)}, u32[]{:S(2)}) copy-start(bf16[5,240,384]{2,1,0:T(8,128)(2,1)} %ens_ref.1) | copy-start | bytes 2764804
  98.3 57.5 %copy-start.1 = (bf16[384,384]{1,0:T(8,128)(2,1)S(1)}, bf16[384,384]{1,0:T(8,128)(2,1)}, u32[]{:S(2)}) copy-start(bf16[384,384]{1,0:T(8,128)(2,1)} %get-tuple-element.8.spread_ref) | copy-start | bytes 884740

commit v5 on v4

--- a/solution.py
+++ b/solution.py
@@ -78,22 +78,18 @@
     return [m * CHANNELS + 2 * group + parity for parity in range(2) for m in range(MEMBERS)]
 
 
-def widen(ens_ref, wide_ref):
-    for m in range(MEMBERS):
-        for j in range(3):
-            rows = slice(m * CHANNELS, (m + 1) * CHANNELS)
-            wide_ref[j, rows, :] = ens_ref[m, :, 128 * j : 128 * j + 128].astype(F32)
-
-
 def source_kernel(mem_ref, *refs):
-    sources, (out_ref, spread_ref), landed, sems = refs[:5], refs[5:7], refs[7:12], refs[12]
-    wide_ref = refs[13]
-    copies = [pltpu.make_async_copy(a, b, sems.at[k]) for k, (a, b) in enumerate(zip(sources, landed))]
-    for copy in copies:
+    ens_hbm, small, (out_hbm, spread_hbm), landed = refs[0], refs[1:5], refs[5:7], refs[8:12]
+    ens_ref, wide_ref, out_ref, spread_ref, in_sems, out_sems = refs[7], *refs[12:17]
+    fetches = [pltpu.make_async_copy(a, b, in_sems.at[k]) for k, (a, b) in enumerate(zip(small, landed))]
+    members = [
+        pltpu.make_async_copy(ens_hbm.at[m], ens_ref.at[m], in_sems.at[4 + m]) for m in range(MEMBERS)
+    ]
+    for copy in fetches + members:
         copy.start()
-    for copy in copies[1:]:
+    for copy in fetches:
         copy.wait()
-    ens_ref, margin_ref, owner_ref, patch_ref, letkf_ref = landed
+    margin_ref, owner_ref, patch_ref, letkf_ref = landed
     lane24 = iota((24, ELEMENTS), 1)
     block_of = (lane24 // 128) * 8 + lane24 % 8
     pick_block = iota((24, ELEMENTS), 0) == block_of
@@ -110,6 +106,8 @@
     sums = jnp.sum(spread, axis=0, keepdims=True)
     spread = spread.astype(BF)
     spread_ref[...] = spread
+    leaving = [pltpu.make_async_copy(spread_ref, spread_hbm, out_sems.at[8])]
+    leaving[0].start()
     high = sums.astype(BF).astype(F32)
     low = sums - high
 
@@ -127,8 +125,11 @@
     sides = [place, high, low] + [weights[n : n + 1] for n in range(MEMBERS)] + [jnp.zeros_like(low)] * 2
     spare = iota((16, ELEMENTS), 0) == 15
 
-    copies[0].wait()
-    widen(ens_ref, wide_ref)
+    for m in range(MEMBERS):
+        members[m].wait()
+        for j in range(3):
+            rows = slice(m * CHANNELS, (m + 1) * CHANNELS)
+            wide_ref[j, rows, :] = ens_ref[m, :, 128 * j : 128 * j + 128].astype(F32)
     for group in range(8):
         tiles = [
             jnp.concatenate([wide_ref[j, pl.ds(start, 16, 16), :] for j in range(3)], axis=1)
@@ -142,6 +143,11 @@
         rest = [pieces[128:160, 128 * h : 128 * h + 128] for h in range(THIRDS)]
         rest = jnp.concatenate(rest + [jnp.zeros((32, 128), F32)], axis=0)
         pack(out_ref, slice(8 * group, 8 * group + 8), firsts, rest.T.reshape(8, ROWS, 128))
+        part = pl.ds(8 * group, 8)
+        leaving.append(pltpu.make_async_copy(out_ref.at[part], out_hbm.at[part], out_sems.at[group]))
+        leaving[-1].start()
+    for copy in leaving:
+        copy.wait()
 
 
 def hits(first):
@@ -219,11 +225,10 @@
     pack(out_ref, every, firsts, last.reshape(MESH, ROWS, 128))
 
 
-def final_kernel(back_ref, ens_ref, spread_ref, out_ref, wide_ref):
+def final_kernel(back_ref, ens_ref, spread_ref, out_hbm, wide_ref, out_ref, sems):
     spread = spread_ref[...]
     area = dot_nt(jnp.ones((16, ELEMENTS), BF), spread)[0:1]
     scale = 1.0 / area
-    widen(ens_ref, wide_ref)
     for group in range(8):
         at = slice(8 * group, 8 * group + 8)
         first = jnp.concatenate([unpack(back_ref, at, h).reshape(128, 128).T for h in range(THIRDS)], axis=1)
@@ -232,26 +237,36 @@
         left = jnp.concatenate([first, last], axis=0).astype(BF)
         correction = dot_nt(left, spread) * scale
         for k, start in enumerate(places(group)):
-            rows = pl.ds(start, 15, 16)
             for j in range(3):
-                change = correction[16 * k : 16 * k + 15, 128 * j : 128 * j + 128]
-                wide_ref[j, rows, :] = wide_ref[j, rows, :] + change
+                wide_ref[j, pl.ds(start, 15, 16), :] = correction[
+                    16 * k : 16 * k + 15, 128 * j : 128 * j + 128
+                ]
+    copies = []
     for m in range(MEMBERS):
         for j in range(3):
             rows = slice(m * CHANNELS, (m + 1) * CHANNELS)
-            out_ref[m, :, 128 * j : 128 * j + 128] = wide_ref[j, rows, :].astype(BF)
+            lanes = slice(128 * j, 128 * j + 128)
+            out_ref[m, :, lanes] = (ens_ref[m, :, lanes].astype(F32) + wide_ref[j, rows, :]).astype(BF)
+        copies.append(pltpu.make_async_copy(out_ref.at[m], out_hbm.at[m], sems.at[m]))
+        copies[-1].start()
+    for copy in copies:
+        copy.wait()
 
 
 def vmem():
     return pl.BlockSpec(memory_space=pltpu.VMEM)
 
 
-def call(kernel, outs, ins, scratch=(), limit=VMEM_BYTES):
+def hbm():
+    return pl.BlockSpec(memory_space=pltpu.HBM)
+
+
+def call(kernel, outs, ins, scratch=(), limit=VMEM_BYTES, place=vmem):
     return pl.pallas_call(
         kernel,
         out_shape=[jax.ShapeDtypeStruct(s, d) for s, d in outs],
         in_specs=ins,
-        out_specs=[vmem() for _ in outs],
+        out_specs=[place() for _ in outs],
         scratch_shapes=list(scratch),
         compiler_params=pltpu.CompilerParams(vmem_limit_bytes=limit),
     )
@@ -263,17 +278,21 @@
     send, spread = call(
         source_kernel,
         [((MESH, QUARTERS, WIDTH), BF), ((ELEMENTS, ELEMENTS), BF)],
-        [pl.BlockSpec(memory_space=pltpu.SMEM)] + [pl.BlockSpec(memory_space=pltpu.HBM)] * 5,
+        [pl.BlockSpec(memory_space=pltpu.SMEM)] + [hbm()] * 5,
         [
             pltpu.VMEM((MEMBERS, CHANNELS, ELEMENTS), BF),
             pltpu.VMEM((256, 24), BF),
             pltpu.VMEM((2, 24), jnp.int32),
             pltpu.VMEM((2, 24), jnp.int32),
             pltpu.VMEM((MEM * MEMBERS, MEM * MEMBERS), F32),
-            pltpu.SemaphoreType.DMA((5,)),
             pltpu.VMEM((3, WIDE_ROWS, 128), F32),
+            pltpu.VMEM((MESH, QUARTERS, WIDTH), BF),
+            pltpu.VMEM((ELEMENTS, ELEMENTS), BF),
+            pltpu.SemaphoreType.DMA((9,)),
+            pltpu.SemaphoreType.DMA((9,)),
         ],
         SOURCE_VMEM_BYTES,
+        hbm,
     )(mem, ensemble, margin, ovl_owner.T, ovl_patch.T, letkf_weight[0])
     got = lax.all_to_all(send, "mesh", split_axis=0, concat_axis=0, tiled=True)
     (fields,) = call(patch_kernel, [((MEM, 96, 128), BF)], [vmem()])(got)
@@ -291,7 +310,12 @@
         final_kernel,
         [((MEMBERS, CHANNELS, ELEMENTS), BF)],
         [vmem()] * 3,
-        [pltpu.VMEM((3, WIDE_ROWS, 128), F32)],
+        [
+            pltpu.VMEM((3, WIDE_ROWS, 128), F32),
+            pltpu.VMEM((MEMBERS, CHANNELS, ELEMENTS), BF),
+            pltpu.SemaphoreType.DMA((MEMBERS,)),
+        ],
+        place=hbm,
     )(returned, ensemble, spread)
     return analysis
 

time: 160 us -> 159 us (level)
  no operation moved by 1% of the time
where the time goes in v5:
time: 159 us; the launch traced here: 158 us
  blocking collectives  147 us (92%)
  Pallas kernels  11.3 us (7%)
    all_to_all x1, blocking collectives, shards(): got = lax.all_to_all(send, 'mesh', split_axis=0, concat_axis=0, tiled=True)  69.8 us
    all_to_all x1, blocking collectives, shards(): lax.all_to_all(back, 'mesh', split_axis=0, concat_axis=0, tiled=True)  57.5 us
    all_to_all x1, blocking collectives, shards(): lax.all_to_all(fields, 'mem', split_axis=0, concat_axis=0, tiled=True)  10.9 us
    all_to_all x1, blocking collectives, shards(): lax.all_to_all(mixed, 'mem', split_axis=0, concat_axis=0, tiled=True)  8.88 us
    pallas_call x1, Pallas kernels, shards(): call(source_kernel, [((MESH, QUARTERS, WIDTH), BF), ((ELEMENTS, ELEMENTS)...  4.13 us

profile of v5, /device:TPU:8, one launch (start us, length us, event | category | flops | bytes accessed | tf_op | source)
XLA Modules:
  0.0 158.5 jit_solution(14768042286135493263)
XLA Ops:
  0.0 4.1 %shard_map.55 = (bf16[64,4,1920]{2,1,0:T(4,128)(2,1)}, bf16[384,384]{1,0:T(8,128)(2,1)}) custom-call(s32[1]{0:T(128)} %bitcast.mem_ref, bf16[5,240,384]{2,1,0:T(8,128)(2,1)} %ens_ref.1, bf16[256,24]{1,0:T(8,128)(2,1)} %bitcast.7, s32[2,24]{1,0:T(2,128)} %bitcast.9, s32[2,24]{1,0:T(2,128)} %bitcast.10, f32[40,40]{1,0:T(8,128)} %bitcast.8), custom_call_target="tpu_custom_call" | custom-call | tf_op jit(solution)/shard_map/pallas_call | solution.py:278
  4.1 69.8 %all_to_all.20.got_ref = bf16[64,4,1920]{2,1,0:T(4,128)(2,1)S(1)} all-to-all(bf16[64,4,1920]{2,1,0:T(4,128)(2,1)} %get-tuple-element.7), channel_id=1, replica_groups=mesh['mesh'=64,'mem'=8] {'mesh'}, dimensions={0} | all-to-all | bytes 1966080 | tf_op jit(solution)/shard_map/all_to_all | solution.py:297
  73.9 1.4 shard_map.56
  75.3 10.9 %all_to_all.21.got_ref = bf16[8,96,128]{2,1,0:T(8,128)(2,1)S(1)} all-to-all(bf16[8,96,128]{2,1,0:T(8,128)(2,1)S(1)} %shard_map.56), channel_id=1, replica_groups=mesh['mesh'=64,'mem'=8] {'mem'}, dimensions={0} | all-to-all | bytes 393216 | tf_op jit(solution)/shard_map/all_to_all | solution.py:299
  86.3 1.4 shard_map.57
  87.7 8.9 %all_to_all.22.inc_ref = bf16[8,80,128]{2,1,0:T(8,128)(2,1)S(1)} all-to-all(bf16[8,80,128]{2,1,0:T(8,128)(2,1)S(1)} %shard_map.57), channel_id=1, replica_groups=mesh['mesh'=64,'mem'=8] {'mem'}, dimensions={0} | all-to-all | bytes 327680 | tf_op jit(solution)/shard_map/all_to_all | solution.py:306
  96.6 1.4 shard_map.58
  97.9 0.0 copy-start
  98.0 0.0 copy-start.1
  98.0 57.5 %all_to_all.23.back_ref = bf16[64,4,1920]{2,1,0:T(4,128)(2,1)S(1)} all-to-all(bf16[64,4,1920]{2,1,0:T(4,128)(2,1)S(1)} %shard_map.58), channel_id=1, replica_groups=mesh['mesh'=64,'mem'=8] {'mesh'}, dimensions={0} | all-to-all | bytes 1966080 | tf_op jit(solution)/shard_map/all_to_all | solution.py:308
  155.5 0.0 copy-done
  155.5 0.0 copy-done.1
  155.5 3.0 %shard_map.59 = bf16[5,240,384]{2,1,0:T(8,128)(2,1)} custom-call(bf16[64,4,1920]{2,1,0:T(4,128)(2,1)S(1)} %all_to_all.23.back_ref, bf16[5,240,384]{2,1,0:T(8,128)(2,1)S(1)} %copy-done, bf16[384,384]{1,0:T(8,128)(2,1)S(1)} %copy-done.1), custom_call_target="tpu_custom_call" | custom-call | tf_op jit(solution)/shard_map/pallas_call | solution.py:309
Async XLA Ops:
  97.9 57.5 %copy-start = (bf16[5,240,384]{2,1,0:T(8,128)(2,1)S(1)}, bf16[5,240,384]{2,1,0:T(8,128)(2,1)}, u32[]{:S(2)}) copy-start(bf16[5,240,384]{2,1,0:T(8,128)(2,1)} %ens_ref.1) | copy-start | bytes 2764804
  98.0 57.5 %copy-start.1 = (bf16[384,384]{1,0:T(8,128)(2,1)S(1)}, bf16[384,384]{1,0:T(8,128)(2,1)}, u32[]{:S(2)}) copy-start(bf16[384,384]{1,0:T(8,128)(2,1)} %get-tuple-element.8.spread_ref) | copy-start | bytes 884740

commit v6 on v5

--- a/solution.py
+++ b/solution.py
@@ -74,13 +74,13 @@
     return jnp.concatenate(tiles + [tail], axis=1)
 
 
-def places(group):
-    return [m * CHANNELS + 2 * group + parity for parity in range(2) for m in range(MEMBERS)]
+def place_of(group, k):
+    return k % MEMBERS * CHANNELS + 2 * group + k // MEMBERS
 
 
 def source_kernel(mem_ref, *refs):
     ens_hbm, small, (out_hbm, spread_hbm), landed = refs[0], refs[1:5], refs[5:7], refs[8:12]
-    ens_ref, wide_ref, out_ref, spread_ref, in_sems, out_sems = refs[7], *refs[12:17]
+    ens_ref, wide_ref, out_ref, spread_ref, side_ref, in_sems, out_sems = refs[7], *refs[12:18]
     fetches = [pltpu.make_async_copy(a, b, in_sems.at[k]) for k, (a, b) in enumerate(zip(small, landed))]
     members = [
         pltpu.make_async_copy(ens_hbm.at[m], ens_ref.at[m], in_sems.at[4 + m]) for m in range(MEMBERS)
@@ -106,8 +106,8 @@
     sums = jnp.sum(spread, axis=0, keepdims=True)
     spread = spread.astype(BF)
     spread_ref[...] = spread
-    leaving = [pltpu.make_async_copy(spread_ref, spread_hbm, out_sems.at[8])]
-    leaving[0].start()
+    leaving = pltpu.make_async_copy(spread_ref, spread_hbm, out_sems.at[8])
+    leaving.start()
     high = sums.astype(BF).astype(F32)
     low = sums - high
 
@@ -122,32 +122,39 @@
     mine = dot_nt(pick_own, letkf_ref[...].astype(BF)).astype(BF)
     lane40 = iota((40, ELEMENTS), 1)
     weights = dot(mine, one_hot(iota((40, ELEMENTS), 0) == (lane40 // 128) * 16 + lane40 % 16))
-    sides = [place, high, low] + [weights[n : n + 1] for n in range(MEMBERS)] + [jnp.zeros_like(low)] * 2
-    spare = iota((16, ELEMENTS), 0) == 15
+    sides = [place, high, low] + [weights[n : n + 1] for n in range(MEMBERS)]
+    side_ref[...] = jnp.concatenate(sides + [jnp.zeros((8, ELEMENTS), F32)], axis=0)
+    spare = iota((16, 128), 0) == 15
 
     for m in range(MEMBERS):
         members[m].wait()
-        for j in range(3):
-            rows = slice(m * CHANNELS, (m + 1) * CHANNELS)
-            wide_ref[j, rows, :] = ens_ref[m, :, 128 * j : 128 * j + 128].astype(F32)
+        pieces = dot(ens_ref[m], spread)
+        for j in range(THIRDS):
+            wide_ref[j, m * CHANNELS : (m + 1) * CHANNELS, :] = pieces[:, 128 * j : 128 * j + 128]
+
+    def group_copy(group):
+        part = pl.ds(8 * group, 8)
+        return pltpu.make_async_copy(out_ref.at[part], out_hbm.at[part], out_sems.at[group])
+
+    def send(group, carry):
+        firsts, rest = [], []
+        for h in range(THIRDS):
+            lanes = slice(128 * h, 128 * h + 128)
+            rows = []
+            for k in range(2 * MEMBERS):
+                tile = wide_ref[h, pl.ds(place_of(group, k), 16, 16), :]
+                rows.append(jnp.where(spare, side_ref[k : k + 1, lanes], tile))
+            firsts.append(jnp.concatenate(rows[:8], axis=0).T.reshape(8, ROWS, 128))
+            rest += rows[8:]
+        rest = jnp.concatenate(rest + [jnp.zeros((32, 128), F32)], axis=0)
+        pack(out_ref, pl.ds(8 * group, 8), firsts, rest.T.reshape(8, ROWS, 128))
+        group_copy(group).start()
+        return carry
+
+    lax.fori_loop(0, 8, send, 0)
+    leaving.wait()
     for group in range(8):
-        tiles = [
-            jnp.concatenate([wide_ref[j, pl.ds(start, 16, 16), :] for j in range(3)], axis=1)
-            for start in places(group)
-        ]
-        pieces = dot(jnp.concatenate(tiles, axis=0).astype(BF), spread)
-        pieces = jnp.concatenate(
-            [jnp.where(spare, sides[k], pieces[16 * k : 16 * k + 16]) for k in range(10)], axis=0
-        )
-        firsts = [pieces[0:128, 128 * h : 128 * h + 128].T.reshape(8, ROWS, 128) for h in range(THIRDS)]
-        rest = [pieces[128:160, 128 * h : 128 * h + 128] for h in range(THIRDS)]
-        rest = jnp.concatenate(rest + [jnp.zeros((32, 128), F32)], axis=0)
-        pack(out_ref, slice(8 * group, 8 * group + 8), firsts, rest.T.reshape(8, ROWS, 128))
-        part = pl.ds(8 * group, 8)
-        leaving.append(pltpu.make_async_copy(out_ref.at[part], out_hbm.at[part], out_sems.at[group]))
-        leaving[-1].start()
-    for copy in leaving:
-        copy.wait()
+        group_copy(group).wait()
 
 
 def hits(first):
@@ -229,18 +236,22 @@
     spread = spread_ref[...]
     area = dot_nt(jnp.ones((16, ELEMENTS), BF), spread)[0:1]
     scale = 1.0 / area
-    for group in range(8):
-        at = slice(8 * group, 8 * group + 8)
+
+    def correct(group, carry):
+        at = pl.ds(8 * group, 8)
         first = jnp.concatenate([unpack(back_ref, at, h).reshape(128, 128).T for h in range(THIRDS)], axis=1)
         last = unpack_last(back_ref, at).reshape(128, 128).T
         last = jnp.concatenate([last[32 * h : 32 * h + 32] for h in range(THIRDS)], axis=1)
         left = jnp.concatenate([first, last], axis=0).astype(BF)
         correction = dot_nt(left, spread) * scale
-        for k, start in enumerate(places(group)):
+        for k in range(2 * MEMBERS):
             for j in range(3):
-                wide_ref[j, pl.ds(start, 15, 16), :] = correction[
+                wide_ref[j, pl.ds(place_of(group, k), 15, 16), :] = correction[
                     16 * k : 16 * k + 15, 128 * j : 128 * j + 128
                 ]
+        return carry
+
+    lax.fori_loop(0, 8, correct, 0)
     copies = []
     for m in range(MEMBERS):
         for j in range(3):
@@ -288,6 +299,7 @@
             pltpu.VMEM((3, WIDE_ROWS, 128), F32),
             pltpu.VMEM((MESH, QUARTERS, WIDTH), BF),
             pltpu.VMEM((ELEMENTS, ELEMENTS), BF),
+            pltpu.VMEM((16, ELEMENTS), F32),
             pltpu.SemaphoreType.DMA((9,)),
             pltpu.SemaphoreType.DMA((9,)),
         ],

time: 159 us -> 161 us (1.013)
  Pallas kernels: 11.3 us -> 13.9 us
where the time goes in v6:
time: 161 us
  blocking collectives  147 us (91%)
  Pallas kernels  13.9 us (9%)
    all_to_all x1, blocking collectives, shards(): got = lax.all_to_all(send, 'mesh', split_axis=0, concat_axis=0, tiled=True)  69.8 us
    all_to_all x1, blocking collectives, shards(): lax.all_to_all(back, 'mesh', split_axis=0, concat_axis=0, tiled=True)  57.5 us
    all_to_all x1, blocking collectives, shards(): lax.all_to_all(fields, 'mem', split_axis=0, concat_axis=0, tiled=True)  10.9 us
    all_to_all x1, blocking collectives, shards(): lax.all_to_all(mixed, 'mem', split_axis=0, concat_axis=0, tiled=True)  8.88 us
    pallas_call x1, Pallas kernels, shards(): call(source_kernel, [((MESH, QUARTERS, WIDTH), BF), ((ELEMENTS, ELEMENTS)...  5.18 us
    pallas_call x1, Pallas kernels, shards(): call(final_kernel, [((MEMBERS, CHANNELS, ELEMENTS), BF)], [vmem()] * 3, [...  4.49 us

profile of v6, /device:TPU:8, one launch (start us, length us, event | category | flops | bytes accessed | tf_op | source)
XLA Modules:
  0.0 161.0 jit_solution(15102176403765320765)
XLA Ops:
  0.0 5.2 %shard_map.55 = (bf16[64,4,1920]{2,1,0:T(4,128)(2,1)}, bf16[384,384]{1,0:T(8,128)(2,1)}) custom-call(s32[1]{0:T(128)} %bitcast.mem_ref, bf16[5,240,384]{2,1,0:T(8,128)(2,1)} %ens_ref.1, bf16[256,24]{1,0:T(8,128)(2,1)} %bitcast.7, s32[2,24]{1,0:T(2,128)} %bitcast.9, s32[2,24]{1,0:T(2,128)} %bitcast.10, f32[40,40]{1,0:T(8,128)} %bitcast.8), custom_call_target="tpu_custom_call" | custom-call | tf_op jit(solution)/shard_map/pallas_call | solution.py:289
  5.2 69.8 %all_to_all.20.got_ref = bf16[64,4,1920]{2,1,0:T(4,128)(2,1)S(1)} all-to-all(bf16[64,4,1920]{2,1,0:T(4,128)(2,1)} %get-tuple-element.7), channel_id=1, replica_groups=mesh['mesh'=64,'mem'=8] {'mesh'}, dimensions={0} | all-to-all | bytes 1966080 | tf_op jit(solution)/shard_map/all_to_all | solution.py:309
  74.9 1.4 shard_map.56
  76.4 10.9 %all_to_all.21.got_ref = bf16[8,96,128]{2,1,0:T(8,128)(2,1)S(1)} all-to-all(bf16[8,96,128]{2,1,0:T(8,128)(2,1)S(1)} %shard_map.56), channel_id=1, replica_groups=mesh['mesh'=64,'mem'=8] {'mem'}, dimensions={0} | all-to-all | bytes 393216 | tf_op jit(solution)/shard_map/all_to_all | solution.py:311
  87.3 1.4 shard_map.57
  88.7 8.9 %all_to_all.22.inc_ref = bf16[8,80,128]{2,1,0:T(8,128)(2,1)S(1)} all-to-all(bf16[8,80,128]{2,1,0:T(8,128)(2,1)S(1)} %shard_map.57), channel_id=1, replica_groups=mesh['mesh'=64,'mem'=8] {'mem'}, dimensions={0} | all-to-all | bytes 327680 | tf_op jit(solution)/shard_map/all_to_all | solution.py:318
  97.6 1.4 shard_map.58
  99.0 0.0 copy-start
  99.0 0.0 copy-start.1
  99.0 57.5 %all_to_all.23.back_ref = bf16[64,4,1920]{2,1,0:T(4,128)(2,1)S(1)} all-to-all(bf16[64,4,1920]{2,1,0:T(4,128)(2,1)S(1)} %shard_map.58), channel_id=1, replica_groups=mesh['mesh'=64,'mem'=8] {'mesh'}, dimensions={0} | all-to-all | bytes 1966080 | tf_op jit(solution)/shard_map/all_to_all | solution.py:320
  156.5 0.0 copy-done
  156.6 0.0 copy-done.1
  156.6 4.5 %shard_map.59 = bf16[5,240,384]{2,1,0:T(8,128)(2,1)} custom-call(bf16[64,4,1920]{2,1,0:T(4,128)(2,1)S(1)} %all_to_all.23.back_ref, bf16[5,240,384]{2,1,0:T(8,128)(2,1)S(1)} %copy-done, bf16[384,384]{1,0:T(8,128)(2,1)S(1)} %copy-done.1), custom_call_target="tpu_custom_call" | custom-call | tf_op jit(solution)/shard_map/pallas_call | solution.py:321
Async XLA Ops:
  99.0 57.6 %copy-start = (bf16[5,240,384]{2,1,0:T(8,128)(2,1)S(1)}, bf16[5,240,384]{2,1,0:T(8,128)(2,1)}, u32[]{:S(2)}) copy-start(bf16[5,240,384]{2,1,0:T(8,128)(2,1)} %ens_ref.1) | copy-start | bytes 2764804
  99.0 57.5 %copy-start.1 = (bf16[384,384]{1,0:T(8,128)(2,1)S(1)}, bf16[384,384]{1,0:T(8,128)(2,1)}, u32[]{:S(2)}) copy-start(bf16[384,384]{1,0:T(8,128)(2,1)} %get-tuple-element.8.spread_ref) | copy-start | bytes 884740

commit v7 on v6

--- a/solution.py
+++ b/solution.py
@@ -106,8 +106,8 @@
     sums = jnp.sum(spread, axis=0, keepdims=True)
     spread = spread.astype(BF)
     spread_ref[...] = spread
-    leaving = pltpu.make_async_copy(spread_ref, spread_hbm, out_sems.at[8])
-    leaving.start()
+    leaving = [pltpu.make_async_copy(spread_ref, spread_hbm, out_sems.at[8])]
+    leaving[0].start()
     high = sums.astype(BF).astype(F32)
     low = sums - high
 
@@ -132,11 +132,7 @@
         for j in range(THIRDS):
             wide_ref[j, m * CHANNELS : (m + 1) * CHANNELS, :] = pieces[:, 128 * j : 128 * j + 128]
 
-    def group_copy(group):
-        part = pl.ds(8 * group, 8)
-        return pltpu.make_async_copy(out_ref.at[part], out_hbm.at[part], out_sems.at[group])
-
-    def send(group, carry):
+    for group in range(8):
         firsts, rest = [], []
         for h in range(THIRDS):
             lanes = slice(128 * h, 128 * h + 128)
@@ -148,13 +144,11 @@
             rest += rows[8:]
         rest = jnp.concatenate(rest + [jnp.zeros((32, 128), F32)], axis=0)
         pack(out_ref, pl.ds(8 * group, 8), firsts, rest.T.reshape(8, ROWS, 128))
-        group_copy(group).start()
-        return carry
-
-    lax.fori_loop(0, 8, send, 0)
-    leaving.wait()
-    for group in range(8):
-        group_copy(group).wait()
+        part = pl.ds(8 * group, 8)
+        leaving.append(pltpu.make_async_copy(out_ref.at[part], out_hbm.at[part], out_sems.at[group]))
+        leaving[-1].start()
+    for copy in leaving:
+        copy.wait()
 
 
 def hits(first):
@@ -236,9 +230,8 @@
     spread = spread_ref[...]
     area = dot_nt(jnp.ones((16, ELEMENTS), BF), spread)[0:1]
     scale = 1.0 / area
-
-    def correct(group, carry):
-        at = pl.ds(8 * group, 8)
+    for group in range(8):
+        at = slice(8 * group, 8 * group + 8)
         first = jnp.concatenate([unpack(back_ref, at, h).reshape(128, 128).T for h in range(THIRDS)], axis=1)
         last = unpack_last(back_ref, at).reshape(128, 128).T
         last = jnp.concatenate([last[32 * h : 32 * h + 32] for h in range(THIRDS)], axis=1)
@@ -249,9 +242,6 @@
                 wide_ref[j, pl.ds(place_of(group, k), 15, 16), :] = correction[
                     16 * k : 16 * k + 15, 128 * j : 128 * j + 128
                 ]
-        return carry
-
-    lax.fori_loop(0, 8, correct, 0)
     copies = []
     for m in range(MEMBERS):
         for j in range(3):

time: 161 us -> 159 us (0.988)
  Pallas kernels: 13.9 us -> 11.9 us
where the time goes in v7:
time: 159 us
  blocking collectives  147 us (92%)
  Pallas kernels  11.9 us (7%)
    all_to_all x1, blocking collectives, shards(): got = lax.all_to_all(send, 'mesh', split_axis=0, concat_axis=0, tiled=True)  69.8 us
    all_to_all x1, blocking collectives, shards(): lax.all_to_all(back, 'mesh', split_axis=0, concat_axis=0, tiled=True)  57.5 us
    all_to_all x1, blocking collectives, shards(): lax.all_to_all(fields, 'mem', split_axis=0, concat_axis=0, tiled=True)  10.9 us
    all_to_all x1, blocking collectives, shards(): lax.all_to_all(mixed, 'mem', split_axis=0, concat_axis=0, tiled=True)  8.88 us
    pallas_call x1, Pallas kernels, shards(): call(source_kernel, [((MESH, QUARTERS, WIDTH), BF), ((ELEMENTS, ELEMENTS)...  4.65 us

profile of v7, /device:TPU:8, one launch (start us, length us, event | category | flops | bytes accessed | tf_op | source)
XLA Modules:
  0.0 159.0 jit_solution(12669446307492599556)
XLA Ops:
  0.0 4.6 %shard_map.55 = (bf16[64,4,1920]{2,1,0:T(4,128)(2,1)}, bf16[384,384]{1,0:T(8,128)(2,1)}) custom-call(s32[1]{0:T(128)} %bitcast.mem_ref, bf16[5,240,384]{2,1,0:T(8,128)(2,1)} %ens_ref.1, bf16[256,24]{1,0:T(8,128)(2,1)} %bitcast.7, s32[2,24]{1,0:T(2,128)} %bitcast.9, s32[2,24]{1,0:T(2,128)} %bitcast.10, f32[40,40]{1,0:T(8,128)} %bitcast.8), custom_call_target="tpu_custom_call" | custom-call | tf_op jit(solution)/shard_map/pallas_call | solution.py:279
  4.7 69.8 %all_to_all.20.got_ref = bf16[64,4,1920]{2,1,0:T(4,128)(2,1)S(1)} all-to-all(bf16[64,4,1920]{2,1,0:T(4,128)(2,1)} %get-tuple-element.7), channel_id=1, replica_groups=mesh['mesh'=64,'mem'=8] {'mesh'}, dimensions={0} | all-to-all | bytes 1966080 | tf_op jit(solution)/shard_map/all_to_all | solution.py:299
  74.4 1.4 shard_map.56
  75.9 10.9 %all_to_all.21.got_ref = bf16[8,96,128]{2,1,0:T(8,128)(2,1)S(1)} all-to-all(bf16[8,96,128]{2,1,0:T(8,128)(2,1)S(1)} %shard_map.56), channel_id=1, replica_groups=mesh['mesh'=64,'mem'=8] {'mem'}, dimensions={0} | all-to-all | bytes 393216 | tf_op jit(solution)/shard_map/all_to_all | solution.py:301
  86.8 1.4 shard_map.57
  88.2 8.9 %all_to_all.22.inc_ref = bf16[8,80,128]{2,1,0:T(8,128)(2,1)S(1)} all-to-all(bf16[8,80,128]{2,1,0:T(8,128)(2,1)S(1)} %shard_map.57), channel_id=1, replica_groups=mesh['mesh'=64,'mem'=8] {'mem'}, dimensions={0} | all-to-all | bytes 327680 | tf_op jit(solution)/shard_map/all_to_all | solution.py:308
  97.1 1.4 shard_map.58
  98.5 0.0 copy-start
  98.5 0.0 copy-start.1
  98.5 57.5 %all_to_all.23.back_ref = bf16[64,4,1920]{2,1,0:T(4,128)(2,1)S(1)} all-to-all(bf16[64,4,1920]{2,1,0:T(4,128)(2,1)S(1)} %shard_map.58), channel_id=1, replica_groups=mesh['mesh'=64,'mem'=8] {'mesh'}, dimensions={0} | all-to-all | bytes 1966080 | tf_op jit(solution)/shard_map/all_to_all | solution.py:310
  156.0 0.0 copy-done
  156.0 0.0 copy-done.1
  156.0 3.0 %shard_map.59 = bf16[5,240,384]{2,1,0:T(8,128)(2,1)} custom-call(bf16[64,4,1920]{2,1,0:T(4,128)(2,1)S(1)} %all_to_all.23.back_ref, bf16[5,240,384]{2,1,0:T(8,128)(2,1)S(1)} %copy-done, bf16[384,384]{1,0:T(8,128)(2,1)S(1)} %copy-done.1), custom_call_target="tpu_custom_call" | custom-call | tf_op jit(solution)/shard_map/pallas_call | solution.py:311
Async XLA Ops:
  98.5 57.5 %copy-start = (bf16[5,240,384]{2,1,0:T(8,128)(2,1)S(1)}, bf16[5,240,384]{2,1,0:T(8,128)(2,1)}, u32[]{:S(2)}) copy-start(bf16[5,240,384]{2,1,0:T(8,128)(2,1)} %ens_ref.1) | copy-start | bytes 2764804
  98.5 57.5 %copy-start.1 = (bf16[384,384]{1,0:T(8,128)(2,1)S(1)}, bf16[384,384]{1,0:T(8,128)(2,1)}, u32[]{:S(2)}) copy-start(bf16[384,384]{1,0:T(8,128)(2,1)} %get-tuple-element.8.spread_ref) | copy-start | bytes 884740

commit v8 on v5

--- a/solution.py
+++ b/solution.py
@@ -130,16 +130,18 @@
         for j in range(3):
             rows = slice(m * CHANNELS, (m + 1) * CHANNELS)
             wide_ref[j, rows, :] = ens_ref[m, :, 128 * j : 128 * j + 128].astype(F32)
+    tiles = [
+        jnp.concatenate([wide_ref[j, pl.ds(start, 16, 16), :] for j in range(3)], axis=1)
+        for group in range(8)
+        for start in places(group)
+    ]
+    product = dot(jnp.concatenate(tiles, axis=0).astype(BF), spread)
     for group in range(8):
-        tiles = [
-            jnp.concatenate([wide_ref[j, pl.ds(start, 16, 16), :] for j in range(3)], axis=1)
-            for start in places(group)
-        ]
-        pieces = dot(jnp.concatenate(tiles, axis=0).astype(BF), spread)
+        pieces = product[160 * group : 160 * group + 160]
         pieces = jnp.concatenate(
             [jnp.where(spare, sides[k], pieces[16 * k : 16 * k + 16]) for k in range(10)], axis=0
         )
-        firsts = [pieces[0:128, 128 * h : 128 * h + 128].T.reshape(8, ROWS, 128) for h in range(THIRDS)]
+        firsts = [pieces[0:128, 128 * h : 128 * h + 128].astype(BF).T.reshape(8, ROWS, 128) for h in range(THIRDS)]
         rest = [pieces[128:160, 128 * h : 128 * h + 128] for h in range(THIRDS)]
         rest = jnp.concatenate(rest + [jnp.zeros((32, 128), F32)], axis=0)
         pack(out_ref, slice(8 * group, 8 * group + 8), firsts, rest.T.reshape(8, ROWS, 128))
@@ -198,9 +200,9 @@
                 mixed[n] = mixed[n] + weight_ref[q, w : w + 1, :] * field
         for n in range(MEMBERS):
             out_ref[q, 16 * n : 16 * n + 16, :] = (mixed[n] - field_ref[q, 16 * n : 16 * n + 16, :]).astype(BF)
-        return carry
-
-    lax.fori_loop(0, MEM, mix, 0)
+
+    for q in range(MEM):
+        mix(q, 0)
 
 
 def expand_kernel(inc_ref, got_ref, out_ref):
@@ -229,23 +231,24 @@
     spread = spread_ref[...]
     area = dot_nt(jnp.ones((16, ELEMENTS), BF), spread)[0:1]
     scale = 1.0 / area
+    lefts = []
     for group in range(8):
         at = slice(8 * group, 8 * group + 8)
-        first = jnp.concatenate([unpack(back_ref, at, h).reshape(128, 128).T for h in range(THIRDS)], axis=1)
+        first = jnp.concatenate([unpack(back_ref, at, h).reshape(128, 128).astype(BF).T for h in range(THIRDS)], axis=1)
         last = unpack_last(back_ref, at).reshape(128, 128).T
         last = jnp.concatenate([last[32 * h : 32 * h + 32] for h in range(THIRDS)], axis=1)
-        left = jnp.concatenate([first, last], axis=0).astype(BF)
-        correction = dot_nt(left, spread) * scale
-        for k, start in enumerate(places(group)):
-            for j in range(3):
-                wide_ref[j, pl.ds(start, 15, 16), :] = correction[
-                    16 * k : 16 * k + 15, 128 * j : 128 * j + 128
-                ]
+        lefts.append(jnp.concatenate([first, last.astype(BF)], axis=0))
+    correction = dot_nt(jnp.concatenate(lefts, axis=0), spread) * scale
     copies = []
     for m in range(MEMBERS):
         for j in range(3):
+            lanes = slice(128 * j, 128 * j + 128)
+            for group in range(8):
+                for parity in range(2):
+                    row = 160 * group + 80 * parity + 16 * m
+                    rows = pl.ds(m * CHANNELS + 2 * group + parity, 15, 16)
+                    wide_ref[j, rows, :] = correction[row : row + 15, lanes]
             rows = slice(m * CHANNELS, (m + 1) * CHANNELS)
-            lanes = slice(128 * j, 128 * j + 128)
             out_ref[m, :, lanes] = (ens_ref[m, :, lanes].astype(F32) + wide_ref[j, rows, :]).astype(BF)
         copies.append(pltpu.make_async_copy(out_ref.at[m], out_hbm.at[m], sems.at[m]))
         copies[-1].start()

time: 159 us -> 158 us (level)
  no operation moved by 1% of the time
where the time goes in v8:
time: 158 us
  blocking collectives  147 us (93%)
  Pallas kernels  10.9 us (7%)
    all_to_all x1, blocking collectives, shards(): got = lax.all_to_all(send, 'mesh', split_axis=0, concat_axis=0, tiled=True)  69.7 us
    all_to_all x1, blocking collectives, shards(): lax.all_to_all(back, 'mesh', split_axis=0, concat_axis=0, tiled=True)  57.5 us
    all_to_all x1, blocking collectives, shards(): lax.all_to_all(fields, 'mem', split_axis=0, concat_axis=0, tiled=True)  10.9 us
    all_to_all x1, blocking collectives, shards(): lax.all_to_all(mixed, 'mem', split_axis=0, concat_axis=0, tiled=True)  8.88 us
    pallas_call x1, Pallas kernels, shards(): call(source_kernel, [((MESH, QUARTERS, WIDTH), BF), ((ELEMENTS, ELEMENTS)...  4.11 us

profile of v8, /device:TPU:8, one launch (start us, length us, event | category | flops | bytes accessed | tf_op | source)
XLA Modules:
  0.0 158.0 jit_solution(9147410841889031678)
XLA Ops:
  0.0 4.1 %shard_map.55 = (bf16[64,4,1920]{2,1,0:T(4,128)(2,1)}, bf16[384,384]{1,0:T(8,128)(2,1)}) custom-call(s32[1]{0:T(128)} %bitcast.mem_ref, bf16[5,240,384]{2,1,0:T(8,128)(2,1)} %ens_ref.1, bf16[256,24]{1,0:T(8,128)(2,1)} %bitcast.7, s32[2,24]{1,0:T(2,128)} %bitcast.9, s32[2,24]{1,0:T(2,128)} %bitcast.10, f32[40,40]{1,0:T(8,128)} %bitcast.8), custom_call_target="tpu_custom_call" | custom-call | tf_op jit(solution)/shard_map/pallas_call | solution.py:281
  4.1 69.7 %all_to_all.20.got_ref = bf16[64,4,1920]{2,1,0:T(4,128)(2,1)S(1)} all-to-all(bf16[64,4,1920]{2,1,0:T(4,128)(2,1)} %get-tuple-element.7), channel_id=1, replica_groups=mesh['mesh'=64,'mem'=8] {'mesh'}, dimensions={0} | all-to-all | bytes 1966080 | tf_op jit(solution)/shard_map/all_to_all | solution.py:300
  73.9 1.4 shard_map.56
  75.3 10.9 %all_to_all.21.got_ref = bf16[8,96,128]{2,1,0:T(8,128)(2,1)S(1)} all-to-all(bf16[8,96,128]{2,1,0:T(8,128)(2,1)S(1)} %shard_map.56), channel_id=1, replica_groups=mesh['mesh'=64,'mem'=8] {'mem'}, dimensions={0} | all-to-all | bytes 393216 | tf_op jit(solution)/shard_map/all_to_all | solution.py:302
  86.3 1.2 shard_map.57
  87.5 8.9 %all_to_all.22.inc_ref = bf16[8,80,128]{2,1,0:T(8,128)(2,1)S(1)} all-to-all(bf16[8,80,128]{2,1,0:T(8,128)(2,1)S(1)} %shard_map.57), channel_id=1, replica_groups=mesh['mesh'=64,'mem'=8] {'mem'}, dimensions={0} | all-to-all | bytes 327680 | tf_op jit(solution)/shard_map/all_to_all | solution.py:309
  96.4 1.4 shard_map.58
  97.7 0.0 copy-start
  97.8 0.0 copy-start.1
  97.8 57.5 %all_to_all.23.back_ref = bf16[64,4,1920]{2,1,0:T(4,128)(2,1)S(1)} all-to-all(bf16[64,4,1920]{2,1,0:T(4,128)(2,1)S(1)} %shard_map.58), channel_id=1, replica_groups=mesh['mesh'=64,'mem'=8] {'mesh'}, dimensions={0} | all-to-all | bytes 1966080 | tf_op jit(solution)/shard_map/all_to_all | solution.py:311
  155.3 0.0 copy-done
  155.3 0.0 copy-done.1
  155.3 2.7 %shard_map.59 = bf16[5,240,384]{2,1,0:T(8,128)(2,1)} custom-call(bf16[64,4,1920]{2,1,0:T(4,128)(2,1)S(1)} %all_to_all.23.back_ref, bf16[5,240,384]{2,1,0:T(8,128)(2,1)S(1)} %copy-done, bf16[384,384]{1,0:T(8,128)(2,1)S(1)} %copy-done.1), custom_call_target="tpu_custom_call" | custom-call | tf_op jit(solution)/shard_map/pallas_call | solution.py:312
Async XLA Ops:
  97.7 57.6 %copy-start = (bf16[5,240,384]{2,1,0:T(8,128)(2,1)S(1)}, bf16[5,240,384]{2,1,0:T(8,128)(2,1)}, u32[]{:S(2)}) copy-start(bf16[5,240,384]{2,1,0:T(8,128)(2,1)} %ens_ref.1) | copy-start | bytes 2764804
  97.8 57.5 %copy-start.1 = (bf16[384,384]{1,0:T(8,128)(2,1)S(1)}, bf16[384,384]{1,0:T(8,128)(2,1)}, u32[]{:S(2)}) copy-start(bf16[384,384]{1,0:T(8,128)(2,1)} %get-tuple-element.8.spread_ref) | copy-start | bytes 884740

commit v9 on v8

--- a/solution.py
+++ b/solution.py
@@ -130,14 +130,15 @@
         for j in range(3):
             rows = slice(m * CHANNELS, (m + 1) * CHANNELS)
             wide_ref[j, rows, :] = ens_ref[m, :, 128 * j : 128 * j + 128].astype(F32)
-    tiles = [
-        jnp.concatenate([wide_ref[j, pl.ds(start, 16, 16), :] for j in range(3)], axis=1)
-        for group in range(8)
-        for start in places(group)
-    ]
-    product = dot(jnp.concatenate(tiles, axis=0).astype(BF), spread)
     for group in range(8):
-        pieces = product[160 * group : 160 * group + 160]
+        if group % 2 == 0:
+            tiles = [
+                jnp.concatenate([wide_ref[j, pl.ds(start, 16, 16), :] for j in range(3)], axis=1)
+                for near in (group, group + 1)
+                for start in places(near)
+            ]
+            product = dot(jnp.concatenate(tiles, axis=0).astype(BF), spread)
+        pieces = product[160 * (group % 2) : 160 * (group % 2) + 160]
         pieces = jnp.concatenate(
             [jnp.where(spare, sides[k], pieces[16 * k : 16 * k + 16]) for k in range(10)], axis=0
         )
@@ -238,16 +239,18 @@
         last = unpack_last(back_ref, at).reshape(128, 128).T
         last = jnp.concatenate([last[32 * h : 32 * h + 32] for h in range(THIRDS)], axis=1)
         lefts.append(jnp.concatenate([first, last.astype(BF)], axis=0))
-    correction = dot_nt(jnp.concatenate(lefts, axis=0), spread) * scale
+    corrections = [
+        dot_nt(jnp.concatenate(lefts[k : k + 2], axis=0), spread) * scale for k in range(0, 8, 2)
+    ]
     copies = []
     for m in range(MEMBERS):
         for j in range(3):
             lanes = slice(128 * j, 128 * j + 128)
             for group in range(8):
                 for parity in range(2):
-                    row = 160 * group + 80 * parity + 16 * m
+                    row = 160 * (group % 2) + 80 * parity + 16 * m
                     rows = pl.ds(m * CHANNELS + 2 * group + parity, 15, 16)
-                    wide_ref[j, rows, :] = correction[row : row + 15, lanes]
+                    wide_ref[j, rows, :] = corrections[group // 2][row : row + 15, lanes]
             rows = slice(m * CHANNELS, (m + 1) * CHANNELS)
             out_ref[m, :, lanes] = (ens_ref[m, :, lanes].astype(F32) + wide_ref[j, rows, :]).astype(BF)
         copies.append(pltpu.make_async_copy(out_ref.at[m], out_hbm.at[m], sems.at[m]))

time: 158 us -> 158 us (level)
  no operation moved by 1% of the time
where the time goes in v9:
time: 158 us
  blocking collectives  147 us (93%)
  Pallas kernels  10.7 us (7%)
    all_to_all x1, blocking collectives, shards(): got = lax.all_to_all(send, 'mesh', split_axis=0, concat_axis=0, tiled=True)  69.8 us
    all_to_all x1, blocking collectives, shards(): lax.all_to_all(back, 'mesh', split_axis=0, concat_axis=0, tiled=True)  57.5 us
    all_to_all x1, blocking collectives, shards(): lax.all_to_all(fields, 'mem', split_axis=0, concat_axis=0, tiled=True)  10.9 us
    all_to_all x1, blocking collectives, shards(): lax.all_to_all(mixed, 'mem', split_axis=0, concat_axis=0, tiled=True)  8.88 us
    pallas_call x1, Pallas kernels, shards(): call(source_kernel, [((MESH, QUARTERS, WIDTH), BF), ((ELEMENTS, ELEMENTS)...  4 us

profile of v9, /device:TPU:8, one launch (start us, length us, event | category | flops | bytes accessed | tf_op | source)
XLA Modules:
  0.0 157.9 jit_solution(18229441612767878898)
XLA Ops:
  0.0 4.0 %shard_map.55 = (bf16[64,4,1920]{2,1,0:T(4,128)(2,1)}, bf16[384,384]{1,0:T(8,128)(2,1)}) custom-call(s32[1]{0:T(128)} %bitcast.mem_ref, bf16[5,240,384]{2,1,0:T(8,128)(2,1)} %ens_ref.1, bf16[256,24]{1,0:T(8,128)(2,1)} %bitcast.7, s32[2,24]{1,0:T(2,128)} %bitcast.9, s32[2,24]{1,0:T(2,128)} %bitcast.10, f32[40,40]{1,0:T(8,128)} %bitcast.8), custom_call_target="tpu_custom_call" | custom-call | tf_op jit(solution)/shard_map/pallas_call | solution.py:284
  4.0 69.8 %all_to_all.20.got_ref = bf16[64,4,1920]{2,1,0:T(4,128)(2,1)S(1)} all-to-all(bf16[64,4,1920]{2,1,0:T(4,128)(2,1)} %get-tuple-element.7), channel_id=1, replica_groups=mesh['mesh'=64,'mem'=8] {'mesh'}, dimensions={0} | all-to-all | bytes 1966080 | tf_op jit(solution)/shard_map/all_to_all | solution.py:303
  73.8 1.4 shard_map.56
  75.2 10.9 %all_to_all.21.got_ref = bf16[8,96,128]{2,1,0:T(8,128)(2,1)S(1)} all-to-all(bf16[8,96,128]{2,1,0:T(8,128)(2,1)S(1)} %shard_map.56), channel_id=1, replica_groups=mesh['mesh'=64,'mem'=8] {'mem'}, dimensions={0} | all-to-all | bytes 393216 | tf_op jit(solution)/shard_map/all_to_all | solution.py:305
  86.1 1.2 shard_map.57
  87.4 8.9 %all_to_all.22.inc_ref = bf16[8,80,128]{2,1,0:T(8,128)(2,1)S(1)} all-to-all(bf16[8,80,128]{2,1,0:T(8,128)(2,1)S(1)} %shard_map.57), channel_id=1, replica_groups=mesh['mesh'=64,'mem'=8] {'mem'}, dimensions={0} | all-to-all | bytes 327680 | tf_op jit(solution)/shard_map/all_to_all | solution.py:312
  96.2 1.4 shard_map.58
  97.6 0.0 copy-start
  97.6 0.0 copy-start.1
  97.6 57.5 %all_to_all.23.back_ref = bf16[64,4,1920]{2,1,0:T(4,128)(2,1)S(1)} all-to-all(bf16[64,4,1920]{2,1,0:T(4,128)(2,1)S(1)} %shard_map.58), channel_id=1, replica_groups=mesh['mesh'=64,'mem'=8] {'mesh'}, dimensions={0} | all-to-all | bytes 1966080 | tf_op jit(solution)/shard_map/all_to_all | solution.py:314
  155.2 0.0 copy-done
  155.2 0.0 copy-done.1
  155.2 2.7 %shard_map.59 = bf16[5,240,384]{2,1,0:T(8,128)(2,1)} custom-call(bf16[64,4,1920]{2,1,0:T(4,128)(2,1)S(1)} %all_to_all.23.back_ref, bf16[5,240,384]{2,1,0:T(8,128)(2,1)S(1)} %copy-done, bf16[384,384]{1,0:T(8,128)(2,1)S(1)} %copy-done.1), custom_call_target="tpu_custom_call" | custom-call | tf_op jit(solution)/shard_map/pallas_call | solution.py:315
Async XLA Ops:
  97.6 57.6 %copy-start = (bf16[5,240,384]{2,1,0:T(8,128)(2,1)S(1)}, bf16[5,240,384]{2,1,0:T(8,128)(2,1)}, u32[]{:S(2)}) copy-start(bf16[5,240,384]{2,1,0:T(8,128)(2,1)} %ens_ref.1) | copy-start | bytes 2764804
  97.6 57.5 %copy-start.1 = (bf16[384,384]{1,0:T(8,128)(2,1)S(1)}, bf16[384,384]{1,0:T(8,128)(2,1)}, u32[]{:S(2)}) copy-start(bf16[384,384]{1,0:T(8,128)(2,1)} %get-tuple-element.8.spread_ref) | copy-start | bytes 884740

commit v10 on v9

--- a/solution.py
+++ b/solution.py
@@ -161,16 +161,16 @@
 
 def patch_kernel(got_ref, out_ref):
     every = slice(0, MESH)
-    last_t = unpack_last(got_ref, every).reshape(MESH * ROWS, 128).T
+    last_t = unpack_last(got_ref, every).reshape(MESH * ROWS, 128).astype(BF).T
     grid = jnp.zeros((160, PATCHES), F32)
     weights = [[None] * THIRDS for _ in range(MEMBERS)]
     for h in range(THIRDS):
         first = unpack(got_ref, every, h).reshape(MESH * ROWS, 128)
-        first_t = first.T
-        left = jnp.concatenate([first_t, last_t[32 * h : 32 * h + 32]], axis=0).astype(BF)
+        first_t = first.astype(BF).T
+        left = jnp.concatenate([first_t, last_t[32 * h : 32 * h + 32]], axis=0)
         grid = grid + dot(left, hits(first))
         for n in range(MEMBERS):
-            weights[n][h] = first_t[63 + 16 * n : 64 + 16 * n]
+            weights[n][h] = first_t[63 + 16 * n : 64 + 16 * n].astype(F32)
     cover = grid[31:32] + grid[47:48]
     weights = sum(weights, []) + [jnp.zeros((1, MESH * ROWS), F32)]
     weights = jnp.concatenate(weights, axis=0).astype(BF)
@@ -213,7 +213,7 @@
         halves[0].append(jnp.concatenate([even[:, 0:64], odd[:, 0:64]], axis=1))
         halves[1].append(jnp.concatenate([even[:, 64:128], odd[:, 64:128]], axis=1))
     inc = jnp.concatenate([jnp.concatenate(half, axis=1) for half in halves], axis=0)
-    first = inc[0:128].T.astype(BF)
+    first = inc[0:128].astype(BF).T
     small = inc[128:160]
     last = jnp.zeros((MESH * ROWS, 128), F32)
     every = slice(0, MESH)
@@ -221,7 +221,7 @@
     for h in range(THIRDS):
         pad = [jnp.zeros((32, PATCHES), F32)] * 4
         pad[h] = small
-        right = jnp.concatenate([first, jnp.concatenate(pad, axis=0).T.astype(BF)], axis=1)
+        right = jnp.concatenate([first, jnp.concatenate(pad, axis=0).astype(BF).T], axis=1)
         back = dot(hits(unpack(got_ref, every, h).reshape(MESH * ROWS, 128)), right)
         firsts.append(back[:, 0:128].reshape(MESH, ROWS, 128))
         last = last + back[:, 128:256]

time: 158 us -> 158 us (level)
  no operation moved by 1% of the time
where the time goes in v10:
time: 158 us
  blocking collectives  147 us (93%)
  Pallas kernels  10.7 us (7%)
    all_to_all x1, blocking collectives, shards(): got = lax.all_to_all(send, 'mesh', split_axis=0, concat_axis=0, tiled=True)  69.8 us
    all_to_all x1, blocking collectives, shards(): lax.all_to_all(back, 'mesh', split_axis=0, concat_axis=0, tiled=True)  57.5 us
    all_to_all x1, blocking collectives, shards(): lax.all_to_all(fields, 'mem', split_axis=0, concat_axis=0, tiled=True)  10.9 us
    all_to_all x1, blocking collectives, shards(): lax.all_to_all(mixed, 'mem', split_axis=0, concat_axis=0, tiled=True)  8.88 us
    pallas_call x1, Pallas kernels, shards(): call(source_kernel, [((MESH, QUARTERS, WIDTH), BF), ((ELEMENTS, ELEMENTS)...  4 us

profile of v10, /device:TPU:8, one launch (start us, length us, event | category | flops | bytes accessed | tf_op | source)
XLA Modules:
  0.0 157.8 jit_solution(12591908744322460055)
XLA Ops:
  0.0 4.0 %shard_map.55 = (bf16[64,4,1920]{2,1,0:T(4,128)(2,1)}, bf16[384,384]{1,0:T(8,128)(2,1)}) custom-call(s32[1]{0:T(128)} %bitcast.mem_ref, bf16[5,240,384]{2,1,0:T(8,128)(2,1)} %ens_ref.1, bf16[256,24]{1,0:T(8,128)(2,1)} %bitcast.7, s32[2,24]{1,0:T(2,128)} %bitcast.9, s32[2,24]{1,0:T(2,128)} %bitcast.10, f32[40,40]{1,0:T(8,128)} %bitcast.8), custom_call_target="tpu_custom_call" | custom-call | tf_op jit(solution)/shard_map/pallas_call | solution.py:284
  4.0 69.8 %all_to_all.20.got_ref = bf16[64,4,1920]{2,1,0:T(4,128)(2,1)S(1)} all-to-all(bf16[64,4,1920]{2,1,0:T(4,128)(2,1)} %get-tuple-element.7), channel_id=1, replica_groups=mesh['mesh'=64,'mem'=8] {'mesh'}, dimensions={0} | all-to-all | bytes 1966080 | tf_op jit(solution)/shard_map/all_to_all | solution.py:303
  73.8 1.4 shard_map.56
  75.2 10.9 %all_to_all.21.got_ref = bf16[8,96,128]{2,1,0:T(8,128)(2,1)S(1)} all-to-all(bf16[8,96,128]{2,1,0:T(8,128)(2,1)S(1)} %shard_map.56), channel_id=1, replica_groups=mesh['mesh'=64,'mem'=8] {'mem'}, dimensions={0} | all-to-all | bytes 393216 | tf_op jit(solution)/shard_map/all_to_all | solution.py:305
  86.1 1.2 shard_map.57
  87.3 8.9 %all_to_all.22.inc_ref = bf16[8,80,128]{2,1,0:T(8,128)(2,1)S(1)} all-to-all(bf16[8,80,128]{2,1,0:T(8,128)(2,1)S(1)} %shard_map.57), channel_id=1, replica_groups=mesh['mesh'=64,'mem'=8] {'mem'}, dimensions={0} | all-to-all | bytes 327680 | tf_op jit(solution)/shard_map/all_to_all | solution.py:312
  96.2 1.3 shard_map.58
  97.6 0.0 copy-start
  97.6 0.0 copy-start.1
  97.6 57.5 %all_to_all.23.back_ref = bf16[64,4,1920]{2,1,0:T(4,128)(2,1)S(1)} all-to-all(bf16[64,4,1920]{2,1,0:T(4,128)(2,1)S(1)} %shard_map.58), channel_id=1, replica_groups=mesh['mesh'=64,'mem'=8] {'mesh'}, dimensions={0} | all-to-all | bytes 1966080 | tf_op jit(solution)/shard_map/all_to_all | solution.py:314
  155.1 0.0 copy-done
  155.1 0.0 copy-done.1
  155.1 2.7 %shard_map.59 = bf16[5,240,384]{2,1,0:T(8,128)(2,1)} custom-call(bf16[64,4,1920]{2,1,0:T(4,128)(2,1)S(1)} %all_to_all.23.back_ref, bf16[5,240,384]{2,1,0:T(8,128)(2,1)S(1)} %copy-done, bf16[384,384]{1,0:T(8,128)(2,1)S(1)} %copy-done.1), custom_call_target="tpu_custom_call" | custom-call | tf_op jit(solution)/shard_map/pallas_call | solution.py:315
Async XLA Ops:
  97.6 57.5 %copy-start = (bf16[5,240,384]{2,1,0:T(8,128)(2,1)S(1)}, bf16[5,240,384]{2,1,0:T(8,128)(2,1)}, u32[]{:S(2)}) copy-start(bf16[5,240,384]{2,1,0:T(8,128)(2,1)} %ens_ref.1) | copy-start | bytes 2764804
  97.6 57.5 %copy-start.1 = (bf16[384,384]{1,0:T(8,128)(2,1)S(1)}, bf16[384,384]{1,0:T(8,128)(2,1)}, u32[]{:S(2)}) copy-start(bf16[384,384]{1,0:T(8,128)(2,1)} %get-tuple-element.8.spread_ref) | copy-start | bytes 884740
